TPU v7x, 32 devices: a whole 2x2x4 slice. The times are simulated.
32 devices in a mesh: section: 2 (over core), tensor: 4 (over y, x), dp: 4 (over z).
Axes of the slice: x: 2, y: 2, z: 4, core: 2. Of those that a mesh axis runs over, the one named last changes fastest.
Arguments:
- tokens: bfloat16 [2048, 640], P('dp'), may hold values from -6 to 6
- segments: int32 [2048], P('dp'), may hold values from 0 to 100255, as said below
- cotangent: bfloat16 [2048, 640], P('dp'), may hold values from -6 to 6
- w_query: bfloat16 [2, 640, 1024], P('section', None, 'tensor'), may hold values from -0.25 to 0.25
- w_key: bfloat16 [2, 640, 256], P('section'), may hold values from -0.25 to 0.25
- w_value: bfloat16 [2, 640, 256], P('section'), may hold values from -0.25 to 0.25
- w_out: bfloat16 [2, 1024, 640], P('section', 'tensor'), may hold values from -0.1875 to 0.1875
- w_gate: bfloat16 [2, 640, 2048], P('section', None, 'tensor'), may hold values from -0.25 to 0.25
- w_up: bfloat16 [2, 640, 2048], P('section', None, 'tensor'), may hold values from -0.25 to 0.25
- w_down: bfloat16 [2, 2048, 640], P('section', 'tensor'), may hold values from -0.125 to 0.125
- norm_gains: float32 [2, 4, 640], P('section'), may hold values from 0.25 to 1.75
- head_gains: float32 [2, 2, 256], P('section'), may hold values from 0.25 to 1.75
Outputs:
- section_out: float32 [2, 2048, 640], P('section', 'dp')
- input_grad: float32 [2, 2048, 640], P('section', 'dp')
- grad_query: float32 [2, 640, 1024], P('section', 'dp', 'tensor')
- grad_key: float32 [2, 640, 256], P('section')
- grad_value: float32 [2, 640, 256], P('section')
- grad_out: float32 [2, 1024, 640], P('section', 'tensor', 'dp')
- grad_gate: float32 [2, 640, 2048], P('section', 'dp', 'tensor')
- grad_up: float32 [2, 640, 2048], P('section', 'dp', 'tensor')
- grad_down: float32 [2, 2048, 640], P('section', 'tensor', 'dp')
- grad_norm_gains: float32 [2, 4, 640], P('section', None, 'dp')
- grad_head_gains: float32 [2, 2, 256], P('section')
Inputs may be any that keep to these rules, and one draw needn't show every extreme that they name: `segments`: split tokens into rows of 256 in order (one micro-batch of one data rank each). In every row the real tokens come first: their ids start at 0 at the row's first token and rise by one at each new sequence, so that each sequence is contiguous; the rest of the row is padding, at least one token, each with its own id 100000 plus its place in the row.
All inputs are finite; a program needn't handle non-finite values.
Results may differ from a plain program's by a relative error of at most 0.025.
Values may be sent and summed in bfloat16 or wider, within the bound.
A program may use at most 128 MiB of HBM per device.

v0:
```python
from functools import partial
import math

import jax
import jax.numpy as jnp
from jax import lax
from jax.sharding import PartitionSpec as P

WINDOW = 512
MB_TOK = 256
MICRO = 2


EPSILON = 1e-06


def passed_along(x, axis, by):
    devices = lax.axis_size(axis)
    pairs = [(i, i + by) for i in range(devices) if 0 <= i + by < devices]
    return lax.ppermute(x, axis, pairs)


def norm_rows(values):
    return values * lax.rsqrt(jnp.mean(values * values, axis=-1, keepdims=True) + EPSILON)


def frequencies(head_width):
    half_width = head_width // 2
    return jnp.exp(
        jnp.arange(half_width, dtype=jnp.float32) * (-2.0 * math.log(10000.0) / head_width)
    )


def rotary(values, angles):
    half_width = values.shape[-1] // 2
    front_half = values[..., :half_width]
    back_half = values[..., half_width:]
    cosine = jnp.cos(angles)
    sine_part = jnp.sin(angles)
    return jnp.concatenate(
        [front_half * cosine - back_half * sine_part, back_half * cosine + front_half * sine_part],
        axis=-1,
    )


def row_layout(doc_ids):
    indices = jnp.arange(doc_ids.shape[0], dtype=jnp.int32)
    same_doc = doc_ids[:, None] == doc_ids[None, :]
    before = indices[None, :] <= indices[:, None]
    positions = jnp.sum((same_doc & before).astype(jnp.int32), axis=1) - 1
    allowed = same_doc & before & (indices[:, None] - indices[None, :] < WINDOW)
    return (allowed, positions)


def dot_last(former, latter):
    return lax.dot_general(
        former, latter, (((1,), (1,)), ((), ())), preferred_element_type=jnp.float32
    )


def dot_first(former, latter):
    return lax.dot_general(
        former, latter, (((0,), (0,)), ((), ())), preferred_element_type=jnp.float32
    )


def pre_norm(layer_in, gain_row):
    return norm_rows(layer_in) * gain_row


def head_prep(angles, queries_raw, keys_raw, query_gain, key_gain):
    queries = rotary(norm_rows(queries_raw) * query_gain, angles[:, None, :])
    key_rows = rotary(norm_rows(keys_raw) * key_gain, angles)
    return (queries, key_rows)


def middle(layer_in, attended, attn_gain, mlp_gain):
    residual = layer_in + norm_rows(attended) * attn_gain
    return (residual, norm_rows(residual) * mlp_gain)


def gated(gate_raw, up_raw):
    return jax.nn.gelu(gate_raw, approximate=True) * up_raw


def closing(residual, mlp_sum, post_gain):
    return residual + norm_rows(mlp_sum) * post_gain


def masked_scores(queries16, keys16, allowed):
    score_scale = queries16.shape[-1] ** (-0.5)
    raw_scores = (
        jnp.einsum("qhd,kd->hqk", queries16, keys16, preferred_element_type=jnp.float32)
        * score_scale
    )
    return jnp.where(allowed[None], raw_scores, -1e30)


def forward(layer_in16, doc_ids, weights):
    w_query, w_key, w_value, w_out, w_gate, w_up, w_down, norm_gains, head_gains = weights
    layer_in = layer_in16.astype(jnp.float32)
    row_count = layer_in.shape[0]
    head_width = w_key.shape[1]
    head_count = w_query.shape[1] // head_width
    allowed, positions = row_layout(doc_ids)
    angles = positions.astype(jnp.float32)[:, None] * frequencies(head_width)[None, :]
    normed = pre_norm(layer_in, norm_gains[0]).astype(jnp.bfloat16)
    queries_raw = jnp.dot(normed, w_query, preferred_element_type=jnp.float32).reshape(
        row_count, head_count, head_width
    )
    keys_raw = jnp.dot(normed, w_key, preferred_element_type=jnp.float32)
    values16 = jnp.dot(normed, w_value, preferred_element_type=jnp.float32).astype(jnp.bfloat16)
    queries, key_rows = head_prep(angles, queries_raw, keys_raw, head_gains[0], head_gains[1])
    queries16 = queries.astype(jnp.bfloat16)
    keys16 = key_rows.astype(jnp.bfloat16)
    scores = masked_scores(queries16, keys16, allowed)
    top_score = jnp.max(scores, axis=-1, keepdims=True)
    exponent = jnp.exp(scores - top_score)
    row_total = jnp.sum(exponent, axis=-1, keepdims=True)
    log_total = top_score + jnp.log(row_total)
    attn_prob16 = (exponent / row_total).astype(jnp.bfloat16)
    mixed_heads = jnp.einsum(
        "hqk,kd->qhd", attn_prob16, values16, preferred_element_type=jnp.float32
    )
    mixed16 = mixed_heads.reshape(row_count, head_count * head_width).astype(jnp.bfloat16)
    attn_part = jnp.dot(mixed16, w_out, preferred_element_type=jnp.float32)
    attn_piece = lax.psum_scatter(attn_part, "tensor", scatter_dimension=0, tiled=True)
    attended = lax.all_gather(attn_piece, "tensor", axis=0, tiled=True)
    residual, normed_mlp = middle(layer_in, attended, norm_gains[1], norm_gains[2])
    normed_mlp16 = normed_mlp.astype(jnp.bfloat16)
    gate_raw = jnp.dot(normed_mlp16, w_gate, preferred_element_type=jnp.float32)
    up_raw = jnp.dot(normed_mlp16, w_up, preferred_element_type=jnp.float32)
    hidden16 = gated(gate_raw, up_raw).astype(jnp.bfloat16)
    mlp_part = jnp.dot(hidden16, w_down, preferred_element_type=jnp.float32)
    mlp_piece = lax.psum_scatter(mlp_part, "tensor", scatter_dimension=0, tiled=True)
    mlp_sum = lax.all_gather(mlp_piece, "tensor", axis=0, tiled=True)
    result = closing(residual, mlp_sum, norm_gains[3])
    kept = (
        layer_in,
        angles,
        allowed,
        normed,
        queries_raw,
        keys_raw,
        queries16,
        keys16,
        values16,
        log_total,
        mixed16,
        attended,
        residual,
        normed_mlp16,
        gate_raw,
        up_raw,
        hidden16,
        mlp_sum,
    )
    return (result, kept)


def backward(grad_in, kept, weights):
    w_query, w_key, w_value, w_out, w_gate, w_up, w_down, norm_gains, head_gains = weights
    (
        layer_in,
        angles,
        allowed,
        normed,
        queries_raw,
        keys_raw,
        queries16,
        keys16,
        values16,
        log_total,
        mixed16,
        attended,
        residual,
        normed_mlp16,
        gate_raw,
        up_raw,
        hidden16,
        mlp_sum,
    ) = kept
    row_count, head_count, head_width = queries_raw.shape
    score_scale = head_width ** (-0.5)
    _, close_back = jax.vjp(closing, residual, mlp_sum, norm_gains[3])
    d_residual, d_mlp, d_post = close_back(grad_in)
    d_mlp16 = d_mlp.astype(jnp.bfloat16)
    d_hidden = dot_last(d_mlp16, w_down)
    g_down = dot_first(hidden16, d_mlp16)
    _, gate_back = jax.vjp(gated, gate_raw, up_raw)
    d_gate, d_up = gate_back(d_hidden)
    d_gate16 = d_gate.astype(jnp.bfloat16)
    d_up16 = d_up.astype(jnp.bfloat16)
    g_gate = dot_first(normed_mlp16, d_gate16)
    g_up = dot_first(normed_mlp16, d_up16)
    mlp_back = dot_last(d_gate16, w_gate) + dot_last(d_up16, w_up)
    mlp_back_piece = lax.psum_scatter(
        mlp_back.astype(jnp.bfloat16), "tensor", scatter_dimension=0, tiled=True
    ).astype(jnp.float32)
    d_normed_mlp = lax.all_gather(
        mlp_back_piece.astype(jnp.bfloat16), "tensor", axis=0, tiled=True
    ).astype(mlp_back_piece.dtype)
    _, middle_back = jax.vjp(middle, layer_in, attended, norm_gains[1], norm_gains[2])
    d_skip, d_attended, d_attn_gain, d_mlp_gain = middle_back((d_residual, d_normed_mlp))
    d_attended16 = d_attended.astype(jnp.bfloat16)
    g_out = dot_first(mixed16, d_attended16)
    d_mixed16 = (
        dot_last(d_attended16, w_out)
        .astype(jnp.bfloat16)
        .reshape(row_count, head_count, head_width)
    )
    scores = masked_scores(queries16, keys16, allowed)
    attn_prob = jnp.exp(scores - log_total)
    attn_prob16 = attn_prob.astype(jnp.bfloat16)
    d_prob = jnp.einsum("qhd,kd->hqk", d_mixed16, values16, preferred_element_type=jnp.float32)
    row_inner = jnp.sum(attn_prob * d_prob, axis=-1, keepdims=True)
    d_scores16 = (attn_prob * (d_prob - row_inner)).astype(jnp.bfloat16)
    d_queries = (
        jnp.einsum("hqk,kd->qhd", d_scores16, keys16, preferred_element_type=jnp.float32)
        * score_scale
    )
    d_keys = (
        jnp.einsum("hqk,qhd->kd", d_scores16, queries16, preferred_element_type=jnp.float32)
        * score_scale
    )
    d_values16 = jnp.einsum(
        "hqk,qhd->kd", attn_prob16, d_mixed16, preferred_element_type=jnp.float32
    ).astype(jnp.bfloat16)
    _, prep_back = jax.vjp(
        partial(head_prep, angles), queries_raw, keys_raw, head_gains[0], head_gains[1]
    )
    d_query_raw, d_key_raw, d_query_gain, d_key_gain = prep_back((d_queries, d_keys))
    d_query16 = d_query_raw.reshape(row_count, head_count * head_width).astype(jnp.bfloat16)
    d_key16 = d_key_raw.astype(jnp.bfloat16)
    g_query = dot_first(normed, d_query16)
    g_key = dot_first(normed, d_key16)
    g_value = dot_first(normed, d_values16)
    attn_back = (
        dot_last(d_query16, w_query) + dot_last(d_key16, w_key) + dot_last(d_values16, w_value)
    )
    attn_back_piece = lax.psum_scatter(
        attn_back.astype(jnp.bfloat16), "tensor", scatter_dimension=0, tiled=True
    ).astype(jnp.float32)
    d_normed = lax.all_gather(
        attn_back_piece.astype(jnp.bfloat16), "tensor", axis=0, tiled=True
    ).astype(attn_back_piece.dtype)
    _, pre_back = jax.vjp(pre_norm, layer_in, norm_gains[0])
    d_branch, d_pre_gain = pre_back(d_normed)
    d_input = d_skip + d_branch
    gain_grads = jnp.stack([d_pre_gain, d_attn_gain, d_mlp_gain, d_post])
    head_grads = jnp.stack([d_query_gain, d_key_gain])
    return (d_input, (g_query, g_key, g_value, g_out, g_gate, g_up, g_down, gain_grads, head_grads))


def per_device(
    tokens,
    segments,
    cotangent,
    w_query,
    w_key,
    w_value,
    w_out,
    w_gate,
    w_up,
    w_down,
    norm_gains,
    head_gains,
):
    section_idx = lax.axis_index("section")
    model_width = tokens.shape[1]
    inputs = tokens.reshape(MICRO, MB_TOK, model_width)
    doc_rows = segments.reshape(MICRO, MB_TOK)
    out_grads = cotangent.reshape(MICRO, MB_TOK, model_width)
    weights = (
        w_query[0],
        w_key[0],
        w_value[0],
        w_out[0],
        w_gate[0],
        w_up[0],
        w_down[0],
        norm_gains[0],
        head_gains[0],
    )
    received = jnp.zeros((MB_TOK, model_width), jnp.bfloat16)
    results = []
    stored = []
    for forward_step in range(MICRO + 1):
        micro_idx = jnp.clip(forward_step - section_idx, 0, MICRO - 1)
        current = jnp.where(section_idx == 0, inputs[min(forward_step, MICRO - 1)], received)
        doc_ids = lax.dynamic_index_in_dim(doc_rows, micro_idx, 0, keepdims=False)
        result, kept = forward(current, doc_ids, weights)
        results.append(result)
        stored.append(kept)
        if forward_step < MICRO:
            received = passed_along(result.astype(jnp.bfloat16), "section", 1)
    incoming = jnp.zeros((MB_TOK, model_width), jnp.bfloat16)
    sent_grads = []
    totals = None
    for backward_step in range(MICRO + 1):
        micro_idx = MICRO - backward_step - section_idx
        active_slot = (micro_idx >= 0) & (micro_idx < MICRO)
        start_grad = jnp.where(
            section_idx == 1, out_grads[max(MICRO - 1 - backward_step, 0)], incoming
        )
        grad_in = jnp.where(active_slot, start_grad.astype(jnp.float32), 0.0)
        d_input, grads = backward(grad_in, stored[MICRO - backward_step], weights)
        sent_grads.append(d_input)
        if totals is None:
            totals = list(grads)
        else:
            totals = [earlier + later for earlier, later in zip(totals, grads)]
        if backward_step < MICRO:
            incoming = passed_along(d_input.astype(jnp.bfloat16), "section", -1)
    g_query, g_key, g_value, g_out, g_gate, g_up, g_down, gain_grads, head_grads = totals
    g_query, g_out, g_gate, g_up, g_down, gain_grads = (
        lax.psum_scatter(
            g_query.astype(jnp.bfloat16), "dp", scatter_dimension=0, tiled=True
        ).astype(jnp.float32),
        lax.psum_scatter(g_out.astype(jnp.bfloat16), "dp", scatter_dimension=1, tiled=True).astype(
            jnp.float32
        ),
        lax.psum_scatter(g_gate.astype(jnp.bfloat16), "dp", scatter_dimension=0, tiled=True).astype(
            jnp.float32
        ),
        lax.psum_scatter(g_up.astype(jnp.bfloat16), "dp", scatter_dimension=0, tiled=True).astype(
            jnp.float32
        ),
        lax.psum_scatter(g_down.astype(jnp.bfloat16), "dp", scatter_dimension=1, tiled=True).astype(
            jnp.float32
        ),
        lax.psum_scatter(
            gain_grads.astype(jnp.bfloat16), "dp", scatter_dimension=1, tiled=True
        ).astype(jnp.float32),
    )
    g_key, g_value, head_grads = lax.psum((g_key, g_value, head_grads), ("tensor", "dp"))
    summed = [g_query, g_key, g_value, g_out, g_gate, g_up, g_down, gain_grads, head_grads]
    section_out = lax.dynamic_slice_in_dim(jnp.stack(results), section_idx, MICRO, 0).reshape(
        1, MICRO * MB_TOK, model_width
    )
    input_grad = lax.dynamic_slice_in_dim(
        jnp.stack(sent_grads[::-1]), section_idx, MICRO, 0
    ).reshape(1, MICRO * MB_TOK, model_width)
    return (
        section_out,
        input_grad,
        summed[0][None],
        summed[1][None],
        summed[2][None],
        summed[3][None],
        summed[4][None],
        summed[5][None],
        summed[6][None],
        summed[7][None],
        summed[8][None],
    )


def solution(mesh):
    return jax.shard_map(
        per_device,
        mesh=mesh,
        in_specs=(
            P("dp", None),
            P("dp"),
            P("dp", None),
            P("section", None, "tensor"),
            P("section", None, None),
            P("section", None, None),
            P("section", "tensor", None),
            P("section", None, "tensor"),
            P("section", None, "tensor"),
            P("section", "tensor", None),
            P("section", None, None),
            P("section", None, None),
        ),
        out_specs=(
            P("section", "dp", None),
            P("section", "dp", None),
            P("section", "dp", "tensor"),
            P("section", None, None),
            P("section", None, None),
            P("section", "tensor", "dp"),
            P("section", "dp", "tensor"),
            P("section", "dp", "tensor"),
            P("section", "tensor", "dp"),
            P("section", None, "dp"),
            P("section", None, None),
        ),
        check_vma=False,
    )
```

profile of v0, /device:TPU:0, one launch (start us, length us, event | category | flops | bytes accessed | tf_op | source)
XLA Modules:
  0.0 807.7 jit_solution(17508691141923537969)
XLA Ops:
  17.4 28.2 %reduce-scatter.21.cloned.1.call-done = f32[64,640]{1,0:T(8,128)} async-done(((f32[256,640]{1,0:T(8,128)}), f32[64,640]{1,0:T(8,128)}) %reduce-scatter.21.cloned.1.call-update) | async-done | bytes 163856 | tf_op jit(solution)/shard_map/reduce_scatter | solution.py:127
  45.6 10.5 %all_gather.36 = f32[256,640]{1,0:T(8,128)S(1)} all-gather(f32[64,640]{1,0:T(8,128)} %reduce-scatter.21.cloned.1.call-done), channel_id=1, replica_groups=mesh['section'=2,'tensor'=4,'dp'=4] {'tensor'}, dimensions={0}, use_global_device_ids=true | all-gather | bytes 819200 | tf_op jit(solution)/shard_map/all_gather | solution.py:128
  61.4 25.5 %reduce-scatter.23.cloned.1.call-done = f32[64,640]{1,0:T(8,128)} async-done(((f32[256,640]{1,0:T(8,128)}), f32[64,640]{1,0:T(8,128)}) %reduce-scatter.23.cloned.1.call-update) | async-done | bytes 163856 | tf_op jit(solution)/shard_map/reduce_scatter | solution.py:135
  86.9 10.5 %all_gather.37 = f32[256,640]{1,0:T(8,128)S(1)} all-gather(f32[64,640]{1,0:T(8,128)} %reduce-scatter.23.cloned.1.call-done), channel_id=1, replica_groups=mesh['section'=2,'tensor'=4,'dp'=4] {'tensor'}, dimensions={0}, use_global_device_ids=true | all-gather | bytes 819200 | tf_op jit(solution)/shard_map/all_gather | solution.py:136
  109.7 25.6 %reduce-scatter.25.cloned.1.call-done = f32[64,640]{1,0:T(8,128)} async-done(((f32[256,640]{1,0:T(8,128)}), f32[64,640]{1,0:T(8,128)}) %reduce-scatter.25.cloned.1.call-update) | async-done | bytes 163856 | tf_op jit(solution)/shard_map/reduce_scatter | solution.py:127
  135.3 10.5 %all_gather.38 = f32[256,640]{1,0:T(8,128)S(1)} all-gather(f32[64,640]{1,0:T(8,128)} %reduce-scatter.25.cloned.1.call-done), channel_id=1, replica_groups=mesh['section'=2,'tensor'=4,'dp'=4] {'tensor'}, dimensions={0}, use_global_device_ids=true | all-gather | bytes 819200 | tf_op jit(solution)/shard_map/all_gather | solution.py:128
  152.3 25.5 %reduce-scatter.27.cloned.1.call-done = f32[64,640]{1,0:T(8,128)} async-done(((f32[256,640]{1,0:T(8,128)}), f32[64,640]{1,0:T(8,128)}) %reduce-scatter.27.cloned.1.call-update) | async-done | bytes 163856 | tf_op jit(solution)/shard_map/reduce_scatter | solution.py:135
  177.8 10.5 %all_gather.39 = f32[256,640]{1,0:T(8,128)S(1)} all-gather(f32[64,640]{1,0:T(8,128)} %reduce-scatter.27.cloned.1.call-done), channel_id=1, replica_groups=mesh['section'=2,'tensor'=4,'dp'=4] {'tensor'}, dimensions={0}, use_global_device_ids=true | all-gather | bytes 819200 | tf_op jit(solution)/shard_map/all_gather | solution.py:136
  207.0 25.5 %reduce-scatter.29.cloned.1.call-done = f32[64,640]{1,0:T(8,128)} async-done(((f32[256,640]{1,0:T(8,128)}), f32[64,640]{1,0:T(8,128)}) %reduce-scatter.29.cloned.1.call-update) | async-done | bytes 163856 | tf_op jit(solution)/shard_map/reduce_scatter | solution.py:127
  232.5 10.5 %all_gather.40 = f32[256,640]{1,0:T(8,128)S(1)} all-gather(f32[64,640]{1,0:T(8,128)} %reduce-scatter.29.cloned.1.call-done), channel_id=1, replica_groups=mesh['section'=2,'tensor'=4,'dp'=4] {'tensor'}, dimensions={0}, use_global_device_ids=true | all-gather | bytes 819200 | tf_op jit(solution)/shard_map/all_gather | solution.py:128
  249.5 25.5 %reduce-scatter.31.cloned.1.call-done = f32[64,640]{1,0:T(8,128)} async-done(((f32[256,640]{1,0:T(8,128)}), f32[64,640]{1,0:T(8,128)}) %reduce-scatter.31.cloned.1.call-update) | async-done | bytes 163856 | tf_op jit(solution)/shard_map/reduce_scatter | solution.py:135
  275.0 10.6 %all_gather.41 = f32[256,640]{1,0:T(8,128)S(1)} all-gather(f32[64,640]{1,0:T(8,128)} %reduce-scatter.31.cloned.1.call-done), channel_id=1, replica_groups=mesh['section'=2,'tensor'=4,'dp'=4] {'tensor'}, dimensions={0}, use_global_device_ids=true | all-gather | bytes 819200 | tf_op jit(solution)/shard_map/all_gather | solution.py:136
  292.3 23.1 %reduce-scatter.33.cloned.1.call-done = bf16[64,640]{1,0:T(8,128)(2,1)} async-done(((bf16[256,640]{1,0:T(8,128)(2,1)}), bf16[64,640]{1,0:T(8,128)(2,1)}) %reduce-scatter.33.cloned.1.call-update) | async-done | bytes 81936 | tf_op jit(solution)/shard_map/reduce_scatter | solution.py:197
  315.5 9.3 %all_gather.42 = bf16[256,640]{1,0:T(8,128)(2,1)S(1)} all-gather(bf16[64,640]{1,0:T(8,128)(2,1)} %reduce-scatter.33.cloned.1.call-done), channel_id=1, replica_groups=mesh['section'=2,'tensor'=4,'dp'=4] {'tensor'}, dimensions={0}, use_global_device_ids=true | all-gather | bytes 409600 | tf_op jit(solution)/shard_map/all_gather | solution.py:200
  336.5 24.4 %reduce-scatter.35.cloned.1.call-done = bf16[64,640]{1,0:T(8,128)(2,1)} async-done(((bf16[256,640]{1,0:T(8,128)(2,1)}), bf16[64,640]{1,0:T(8,128)(2,1)}) %reduce-scatter.35.cloned.1.call-update) | async-done | bytes 81936 | tf_op jit(solution)/shard_map/reduce_scatter | solution.py:241
  360.9 9.3 %all_gather.43 = bf16[256,640]{1,0:T(8,128)(2,1)S(1)} all-gather(bf16[64,640]{1,0:T(8,128)(2,1)} %reduce-scatter.35.cloned.1.call-done), channel_id=1, replica_groups=mesh['section'=2,'tensor'=4,'dp'=4] {'tensor'}, dimensions={0}, use_global_device_ids=true | all-gather | bytes 409600 | tf_op jit(solution)/shard_map/all_gather | solution.py:244
  384.4 23.2 %reduce-scatter.37.cloned.1.call-done = bf16[64,640]{1,0:T(8,128)(2,1)} async-done(((bf16[256,640]{1,0:T(8,128)(2,1)}), bf16[64,640]{1,0:T(8,128)(2,1)}) %reduce-scatter.37.cloned.1.call-update) | async-done | bytes 81936 | tf_op jit(solution)/shard_map/reduce_scatter | solution.py:197
  407.6 9.3 %all_gather.44 = bf16[256,640]{1,0:T(8,128)(2,1)S(1)} all-gather(bf16[64,640]{1,0:T(8,128)(2,1)} %reduce-scatter.37.cloned.1.call-done), channel_id=1, replica_groups=mesh['section'=2,'tensor'=4,'dp'=4] {'tensor'}, dimensions={0}, use_global_device_ids=true | all-gather | bytes 409600 | tf_op jit(solution)/shard_map/all_gather | solution.py:200
  428.5 24.4 %reduce-scatter.39.cloned.1.call-done = bf16[64,640]{1,0:T(8,128)(2,1)} async-done(((bf16[256,640]{1,0:T(8,128)(2,1)}), bf16[64,640]{1,0:T(8,128)(2,1)}) %reduce-scatter.39.cloned.1.call-update) | async-done | bytes 81936 | tf_op jit(solution)/shard_map/reduce_scatter | solution.py:241
  453.0 9.3 %all_gather.45 = bf16[256,640]{1,0:T(8,128)(2,1)S(1)} all-gather(bf16[64,640]{1,0:T(8,128)(2,1)} %reduce-scatter.39.cloned.1.call-done), channel_id=1, replica_groups=mesh['section'=2,'tensor'=4,'dp'=4] {'tensor'}, dimensions={0}, use_global_device_ids=true | all-gather | bytes 409600 | tf_op jit(solution)/shard_map/all_gather | solution.py:244
  468.0 2.5 collective-permute-done.3
  477.1 23.1 %reduce-scatter.41.cloned.1.call-done = bf16[64,640]{1,0:T(8,128)(2,1)} async-done(((bf16[256,640]{1,0:T(8,128)(2,1)}), bf16[64,640]{1,0:T(8,128)(2,1)}) %reduce-scatter.41.cloned.1.call-update) | async-done | bytes 81936 | tf_op jit(solution)/shard_map/reduce_scatter | solution.py:197
  500.3 9.5 %all_gather.46 = bf16[256,640]{1,0:T(8,128)(2,1)S(1)} all-gather(bf16[64,640]{1,0:T(8,128)(2,1)} %reduce-scatter.41.cloned.1.call-done), channel_id=1, replica_groups=mesh['section'=2,'tensor'=4,'dp'=4] {'tensor'}, dimensions={0}, use_global_device_ids=true | all-gather | bytes 409600 | tf_op jit(solution)/shard_map/all_gather | solution.py:200
  533.1 2.8 fusion.6
  545.5 9.2 %all_gather.47 = bf16[256,640]{1,0:T(8,128)(2,1)S(1)} all-gather(bf16[64,640]{1,0:T(8,128)(2,1)} %reduce-scatter.43.cloned.1.call-done), channel_id=1, replica_groups=mesh['section'=2,'tensor'=4,'dp'=4] {'tensor'}, dimensions={0}, use_global_device_ids=true | all-gather | bytes 409600 | tf_op jit(solution)/shard_map/all_gather | solution.py:244
  556.0 41.7 %psum.23 = f32[1,2,256]{2,1,0:T(2,128)} all-reduce(f32[1,2,256]{2,1,0:T(2,128)S(1)} %fusion.307), channel_id=1, replica_groups=mesh['section'=2,'tensor'=4,'dp'=4] {'tensor','dp'}, use_global_device_ids=true, to_apply=%region_86.87 | all-reduce | flops 512 | bytes 4096 | tf_op jit(solution)/shard_map/psum | solution.py:336
  599.6 2.5 fusion.4
  603.7 8.0 reduce-scatter.53.cloned.1.call-done
  613.3 21.6 %reduce-scatter.51.cloned.1.call-done = bf16[160,512]{1,0:T(8,128)(2,1)} async-done(((bf16[640,512]{1,0:T(8,128)(2,1)}), bf16[160,512]{1,0:T(8,128)(2,1)}) %reduce-scatter.51.cloned.1.call-update) | async-done | bytes 163856 | tf_op jit(solution)/shard_map/reduce_scatter | solution.py:326
  636.6 21.5 %reduce-scatter.49.cloned.1.call-done = bf16[160,512]{1,0:T(8,128)(2,1)} async-done(((bf16[640,512]{1,0:T(8,128)(2,1)}), bf16[160,512]{1,0:T(8,128)(2,1)}) %reduce-scatter.49.cloned.1.call-update) | async-done | bytes 163856 | tf_op jit(solution)/shard_map/reduce_scatter | solution.py:323
  659.8 18.6 %reduce-scatter.55.cloned.1.call-done = bf16[160,4]{1,0:T(8,128)(2,1)} async-done(((bf16[640,4]{1,0:T(8,128)(2,1)}), bf16[160,4]{1,0:T(8,128)(2,1)}) %reduce-scatter.55.cloned.1.call-update) | async-done | bytes 1296
  679.9 118.3 %all-reduce.15.cloned.1.call-done = (f32[1,640,256]{2,1,0:T(8,128)}, f32[1,640,256]{2,1,0:T(8,128)}) async-done(((f32[1,640,256]{2,1,0:T(8,128)}, f32[1,640,256]{2,1,0:T(8,128)}), (f32[1,640,256]{2,1,0:T(8,128)}, f32[1,640,256]{2,1,0:T(8,128)})) %all-reduce.15.cloned.1.call-update) | async-done | bytes 1310736 | tf_op jit(solution)/shard_map/psum | solution.py:336
  (868 shorter events, 159.2 us)
Async XLA Ops:
  7.2 52.9 %copy-start = (bf16[1,512,640]{2,1,0:T(8,128)(2,1)S(1)}, bf16[1,512,640]{2,1,0:T(8,128)(2,1)}, u32[]{:S(2)}) copy-start(bf16[1,512,640]{2,1,0:T(8,128)(2,1)} %param.21) | copy-start | bytes 1966084
  7.2 38.3 %reduce-scatter.21.cloned.1.call-start = ((), (), s32[]{:S(2)}) async-start(), calls=%async_computation.18 | async-start | bytes 819200 | tf_op jit(solution)/shard_map/reduce_scatter | solution.py:127
  17.3 69.6 %reduce-scatter.23.cloned.1.call-start = ((), (), s32[]{:S(2)}) async-start(), calls=%async_computation.19 | async-start | bytes 819200 | tf_op jit(solution)/shard_map/reduce_scatter | solution.py:135
  57.6 40.0 %copy-start.6 = (f32[256,640]{1,0:T(8,128)}, f32[256,640]{1,0:T(8,128)S(1)}, u32[]{:S(2)}) copy-start(f32[256,640]{1,0:T(8,128)S(1)} %get-tuple-element.67) | copy-start | bytes 1966084
  60.1 37.3 %copy-start.110 = (bf16[256,512]{1,0:T(8,128)(2,1)}, bf16[256,512]{1,0:T(8,128)(2,1)S(1)}, u32[]{:S(2)}) copy-start(bf16[256,512]{1,0:T(8,128)(2,1)S(1)} %get-tuple-element.119) | copy-start | bytes 786436
  61.3 74.0 %reduce-scatter.25.cloned.1.call-start = ((), (), s32[]{:S(2)}) async-start(), calls=%async_computation.20 | async-start | bytes 819200 | tf_op jit(solution)/shard_map/reduce_scatter | solution.py:127
  99.2 2.7 collective-permute-start
  108.5 37.4 %copy-start.134 = (bf16[256,256]{0,1:T(8,128)(2,1)}, bf16[256,256]{0,1:T(8,128)(2,1)S(1)}, u32[]{:S(2)}) copy-start(bf16[256,256]{0,1:T(8,128)(2,1)S(1)} %fusion.27) | copy-start | bytes 393220
  109.7 68.1 %reduce-scatter.27.cloned.1.call-start = ((), (), s32[]{:S(2)}) async-start(), calls=%async_computation.21 | async-start | bytes 819200 | tf_op jit(solution)/shard_map/reduce_scatter | solution.py:135
  147.7 41.4 %copy-start.8 = (f32[256,640]{1,0:T(8,128)}, f32[256,640]{1,0:T(8,128)S(1)}, u32[]{:S(2)}) copy-start(f32[256,640]{1,0:T(8,128)S(1)} %get-tuple-element.63) | copy-start | bytes 1966084
  152.2 80.3 %reduce-scatter.29.cloned.1.call-start = ((), (), s32[]{:S(2)}) async-start(), calls=%async_computation.22 | async-start | bytes 819200 | tf_op jit(solution)/shard_map/reduce_scatter | solution.py:127
  190.2 2.7 collective-permute-start.1
  206.9 68.1 %reduce-scatter.31.cloned.1.call-start = ((), (), s32[]{:S(2)}) async-start(), calls=%async_computation.23 | async-start | bytes 819200 | tf_op jit(solution)/shard_map/reduce_scatter | solution.py:135
  249.4 66.0 %reduce-scatter.33.cloned.1.call-start = ((), (), s32[]{:S(2)}) async-start(), calls=%async_computation.24 | async-start | bytes 409600 | tf_op jit(solution)/shard_map/reduce_scatter | solution.py:197
  291.0 69.9 %reduce-scatter.35.cloned.1.call-start = ((), (), s32[]{:S(2)}) async-start(), calls=%async_computation.25 | async-start | bytes 409600 | tf_op jit(solution)/shard_map/reduce_scatter | solution.py:241
  335.4 34.8 %copy-start.190 = (f32[256]{0:T(256)S(1)}, f32[256]{0:T(256)}, u32[]{:S(2)}) copy-start(f32[256]{0:T(256)} %copy-done.189) | copy-start | bytes 3076
  336.4 71.1 %reduce-scatter.37.cloned.1.call-start = ((), (), s32[]{:S(2)}) async-start(), calls=%async_computation.26 | async-start | bytes 409600 | tf_op jit(solution)/shard_map/reduce_scatter | solution.py:197
  374.0 3.9 collective-permute-start.2
  383.1 69.9 %reduce-scatter.39.cloned.1.call-start = ((), (), s32[]{:S(2)}) async-start(), calls=%async_computation.27 | async-start | bytes 409600 | tf_op jit(solution)/shard_map/reduce_scatter | solution.py:241
  428.5 71.8 %reduce-scatter.41.cloned.1.call-start = ((), (), s32[]{:S(2)}) async-start(), calls=%async_computation.28 | async-start | bytes 409600 | tf_op jit(solution)/shard_map/reduce_scatter | solution.py:197
  466.7 3.9 collective-permute-start.3
  474.7 35.1 %copy-start.7 = (f32[256,640]{1,0:T(8,128)S(1)}, f32[256,640]{1,0:T(8,128)}, u32[]{:S(2)}) copy-start(f32[256,640]{1,0:T(8,128)} %copy-done.6) | copy-start | bytes 1966084
  475.8 69.7 %reduce-scatter.43.cloned.1.call-start = ((), (), s32[]{:S(2)}) async-start(), calls=%async_computation.29 | async-start | bytes 409600 | tf_op jit(solution)/shard_map/reduce_scatter | solution.py:241
  521.1 77.0 %reduce-scatter.47.cloned.1.call-start = ((), (), s32[]{:S(2)}) async-start(), calls=%async_computation.31 | async-start | bytes 409600 | tf_op jit(solution)/shard_map/reduce_scatter | solution.py:320
  523.2 79.0 %reduce-scatter.45.cloned.1.call-start = ((), (), s32[]{:S(2)}) async-start(), calls=%async_computation.30 | async-start | bytes 409600 | tf_op jit(solution)/shard_map/reduce_scatter | solution.py:317
  525.4 86.3 %reduce-scatter.53.cloned.1.call-start = ((), (), s32[]{:S(2)}) async-start(), calls=%async_computation.34 | async-start | bytes 819200 | tf_op jit(solution)/shard_map/reduce_scatter | solution.py:329
  529.7 105.3 %reduce-scatter.51.cloned.1.call-start = ((), (), s32[]{:S(2)}) async-start(), calls=%async_computation.33 | async-start | bytes 819200 | tf_op jit(solution)/shard_map/reduce_scatter | solution.py:326
  533.0 125.1 %reduce-scatter.49.cloned.1.call-start = ((), (), s32[]{:S(2)}) async-start(), calls=%async_computation.32 | async-start | bytes 819200 | tf_op jit(solution)/shard_map/reduce_scatter | solution.py:323
  539.3 139.0 %reduce-scatter.55.cloned.1.call-start = ((), (), s32[]{:S(2)}) async-start(), calls=%async_computation.35 | async-start | bytes 204800
  544.1 53.7 %copy-start.244 = (f32[256]{0:T(256)S(1)}, f32[256]{0:T(256)}, u32[]{:S(2)}) copy-start(f32[256]{0:T(256)} %copy-done.243) | copy-start | bytes 3076
  544.1 53.7 %copy-start.29 = (f32[256,640]{1,0:T(8,128)S(1)}, f32[256,640]{1,0:T(8,128)}, u32[]{:S(2)}) copy-start(f32[256,640]{1,0:T(8,128)} %copy-done.28) | copy-start | bytes 1966084
  555.9 242.3 %all-reduce.15.cloned.1.call-start = ((), (), s32[]{:S(2)}) async-start(), calls=%async_computation.36 | async-start | bytes 2621440 | tf_op jit(solution)/shard_map/psum | solution.py:336
  (286 other events, 841.3 us)
Sparse Core Ops, SparseCore 0:
  17.4 28.1 reduce-scatter.20
  61.4 25.3 reduce-scatter.22
  109.8 25.4 reduce-scatter.24
  152.3 25.4 reduce-scatter.26
  207.0 25.4 reduce-scatter.28
  249.6 25.4 reduce-scatter.30
  291.1 24.2 reduce-scatter.32
  336.5 24.2 reduce-scatter.34
  383.2 24.2 reduce-scatter.36
  428.6 24.2 reduce-scatter.38
  475.9 24.2 reduce-scatter.40
  521.2 24.2 reduce-scatter.42
  547.8 20.1 reduce-scatter.46
  570.7 18.3 reduce-scatter.44
  591.2 20.3 reduce-scatter.52
  613.8 21.0 reduce-scatter.50
  637.0 21.0 reduce-scatter.48
  660.2 18.1 reduce-scatter.54
  685.3 112.7 all-reduce.14
where the time goes:
time: 818 us; the launch traced here: 808 us
  waiting for transfers between devices  470 us (57%)
  blocking collectives  160 us (20%)
  other arithmetic  69.5 us (8%)
  matrix products  54.4 us (7%)
  local copies, waits for them, and re-layouts  28.7 us (4%)
  between operations  18.2 us (2%)
    psum x1, waiting for transfers between devices, per_device(): lax.psum((g_key, g_value, head_grads), ('tensor', 'dp'))  118 us
    reduce_scatter x3, waiting for transfers between devices, forward(): lax.psum_scatter(attn_part, 'tensor', scatter_dimension=0, tiled=True)  79.3 us
    reduce_scatter x3, waiting for transfers between devices, forward(): lax.psum_scatter(mlp_part, 'tensor', scatter_dimension=0, tiled=True)  76.6 us
    reduce_scatter x3, waiting for transfers between devices, backward(): lax.psum_scatter(mlp_back.astype(jnp.bfloat16), 'tensor', scatter_dimensi...  69.4 us
    reduce_scatter x3, waiting for transfers between devices, backward(): lax.psum_scatter(attn_back.astype(jnp.bfloat16), 'tensor', scatter_dimens...  50.3 us
    psum x1, blocking collectives, per_device(): lax.psum((g_key, g_value, head_grads), ('tensor', 'dp'))  41.7 us
    all_gather x3, blocking collectives, forward(): mlp_sum = lax.all_gather(mlp_piece, 'tensor', axis=0, tiled=True)  31.5 us
    all_gather x3, blocking collectives, forward(): attended = lax.all_gather(attn_piece, 'tensor', axis=0, tiled=True)  31.4 us
  transfers between devices with their start and end apart: 23, of which 21 were waited for; matrix products, arithmetic and copies ran while one was open for 5% of the time, Pallas kernels for 0%

commit v1 on v0

v1 whole, which is shorter than its diff:
```python
import functools
import math

import jax
import jax.numpy as jnp
from jax import lax
from jax.experimental import pallas as pl
from jax.experimental.pallas import tpu as pltpu
from jax.sharding import PartitionSpec as P

WINDOW = 512
MB_TOK = 256
EPSILON = 1e-06
BF = jnp.bfloat16
F32 = jnp.float32
MESH = pl.DeviceIdType.MESH
VM = pl.BlockSpec(memory_space=pltpu.VMEM)
ANY = pl.BlockSpec(memory_space=pl.ANY)
VMEM_LIMIT = 50 * 1024 * 1024


def mm(a, b):
    return lax.dot_general(a, b, (((1,), (0,)), ((), ())), preferred_element_type=F32)


def mm_t(a, b):
    return lax.dot_general(a, b, (((1,), (1,)), ((), ())), preferred_element_type=F32)


def t_mm(a, b):
    return lax.dot_general(a, b, (((0,), (0,)), ((), ())), preferred_element_type=F32)


def inverse_rms(v):
    return lax.rsqrt(jnp.mean(v * v, axis=-1, keepdims=True) + EPSILON)


def rms(v):
    return v * inverse_rms(v)


def rms_back(v, gain, cot):
    inv = inverse_rms(v)
    unit = v * inv
    weighted = cot * gain
    d_v = inv * (weighted - unit * jnp.mean(weighted * unit, axis=-1, keepdims=True))
    return d_v, jnp.sum(cot * unit, axis=0, keepdims=True)


def rope(u, cos, sin):
    half = u.shape[-1] // 2
    a, b = u[:, :half], u[:, half:]
    return jnp.concatenate([a * cos - b * sin, b * cos + a * sin], axis=-1)


def rope_back(d, cos, sin):
    half = d.shape[-1] // 2
    a, b = d[:, :half], d[:, half:]
    return jnp.concatenate([a * cos + b * sin, b * cos - a * sin], axis=-1)


GELU_C = math.sqrt(2.0 / math.pi)


def gelu_parts(g):
    th = jnp.tanh(GELU_C * (g + 0.044715 * g * g * g))
    value = 0.5 * g * (1.0 + th)
    slope = 0.5 * (1.0 + th) + 0.5 * g * (1.0 - th * th) * GELU_C * (1.0 + 3 * 0.044715 * g * g)
    return value, slope


def call_exchange(ins, out_shapes, gathered, pre, during, shard, ranks, collective_id):
    n_in, n_out = len(ins), len(out_shapes)
    rows, width = MB_TOK, ins[0].shape[-1]
    share = rows // ranks

    def kernel(*refs):
        in_refs = refs[:n_in]
        gat = refs[n_in : n_in + gathered]
        outs = refs[n_in + gathered : n_in + gathered + n_out]
        part, recv, rs_send, rs_recv, ag_send, ag_recv = refs[n_in + gathered + n_out :]
        me = lax.axis_index("tensor")
        peers = [lax.rem(me + d, ranks) for d in range(1, ranks)]
        barrier = pltpu.get_barrier_semaphore()
        for peer in peers:
            pl.semaphore_signal(barrier, inc=1, device_id={"tensor": peer}, device_id_type=MESH)
        own = pl.ds(pl.multiple_of(me * share, share), share)
        part[...] = pre(in_refs, outs).astype(BF)
        pl.semaphore_wait(barrier, ranks - 1)
        copies = []
        for d, peer in enumerate(peers):
            copy = pltpu.make_async_remote_copy(
                src_ref=part.at[pl.ds(pl.multiple_of(peer * share, share), share)],
                dst_ref=recv.at[d],
                send_sem=rs_send.at[d],
                recv_sem=rs_recv.at[d],
                device_id={"tensor": peer},
                device_id_type=MESH,
            )
            copy.start()
            copies.append(copy)
        if during is not None:
            during(in_refs, outs)
        total = part[own].astype(F32)
        for d, copy in enumerate(copies):
            copy.wait_recv()
            total = total + recv[d].astype(F32)
        results = shard(total, own, in_refs, outs)
        sends = []
        for i in range(gathered):
            gat[i][own] = results[i]
            for d, peer in enumerate(peers):
                copy = pltpu.make_async_remote_copy(
                    src_ref=gat[i].at[own],
                    dst_ref=gat[i].at[own],
                    send_sem=ag_send.at[i, d],
                    recv_sem=ag_recv.at[i, d],
                    device_id={"tensor": peer},
                    device_id_type=MESH,
                )
                copy.start()
                sends.append(copy)
        for copy in copies:
            copy.wait_send()
        for copy in sends:
            copy.wait()

    return pl.pallas_call(
        kernel,
        out_shape=[jax.ShapeDtypeStruct((rows, width), BF)] * gathered + out_shapes,
        in_specs=[VM] * n_in,
        out_specs=[VM] * (gathered + n_out),
        scratch_shapes=[
            pltpu.VMEM((rows, width), BF),
            pltpu.VMEM((ranks - 1, share, width), BF),
            pltpu.SemaphoreType.DMA((ranks - 1,)),
            pltpu.SemaphoreType.DMA((ranks - 1,)),
            pltpu.SemaphoreType.DMA((gathered, ranks - 1)),
            pltpu.SemaphoreType.DMA((gathered, ranks - 1)),
        ],
        compiler_params=pltpu.CompilerParams(
            collective_id=collective_id, has_side_effects=True, vmem_limit_bytes=VMEM_LIMIT
        ),
    )(*ins)


def swap_kernel(count, *refs):
    ins, firsts, seconds = refs[:count], refs[count : 2 * count], refs[2 * count : 3 * count]
    local_sem, send_sem, recv_sem = refs[3 * count :]
    me = lax.axis_index("section")
    other = 1 - me
    barrier = pltpu.get_barrier_semaphore()
    pl.semaphore_signal(barrier, inc=1, device_id={"section": other}, device_id_type=MESH)
    pl.semaphore_wait(barrier, 1)
    for sec, outs in ((0, firsts), (1, seconds)):

        @pl.when(me == sec)
        def _():
            copies = []
            for i in range(count):
                far = pltpu.make_async_remote_copy(
                    src_ref=ins[i],
                    dst_ref=outs[i],
                    send_sem=send_sem.at[i],
                    recv_sem=recv_sem.at[i],
                    device_id={"section": other},
                    device_id_type=MESH,
                )
                near = pltpu.make_async_copy(ins[i], outs[i], local_sem.at[i])
                far.start()
                near.start()
                copies += [far, near]
            for copy in copies:
                copy.wait()


def both_layers(weights):
    count = len(weights)
    shapes = [jax.ShapeDtypeStruct(w.shape, w.dtype) for w in weights]
    outs = pl.pallas_call(
        functools.partial(swap_kernel, count),
        out_shape=shapes * 2,
        in_specs=[ANY] * count,
        out_specs=[ANY] * (2 * count),
        scratch_shapes=[pltpu.SemaphoreType.DMA((count,))] * 3,
        compiler_params=pltpu.CompilerParams(collective_id=1, has_side_effects=True),
    )(*weights)
    return outs[:count], outs[count:]


def struct(shape, dtype=F32):
    return jax.ShapeDtypeStruct(shape, dtype)


def attend_forward(x16, w, tables, ranks, cid):
    w_query, w_key, w_value, w_out, _, _, _, norm_gains, head_gains = w
    cos, sin, seg_col, seg_row = tables
    width = x16.shape[1]
    hd = w_key.shape[-1]
    rows = MB_TOK

    def pre(i, o):
        x_ref, wq, wk, wv, wo, ng, hg, cos, sin, sc, sr = i
        n1_o, qr_o, kr_o, q_o, k_o, v_o, p_o, mix_o = o[:8]
        n1 = (rms(x_ref[...].astype(F32)) * ng[0, 0:1]).astype(BF)
        n1_o[...] = n1
        qr = mm(n1, wq[0])
        kr = mm(n1, wk[0])
        v = mm(n1, wv[0]).astype(BF)
        qr_o[...] = qr
        kr_o[...] = kr
        v_o[...] = v
        q = rope(rms(qr) * hg[0, 0:1], cos[...], sin[...]).astype(BF)
        k = rope(rms(kr) * hg[0, 1:2], cos[...], sin[...]).astype(BF)
        q_o[...] = q
        k_o[...] = k
        at = lax.broadcasted_iota(jnp.int32, (rows, rows), 0)
        to = lax.broadcasted_iota(jnp.int32, (rows, rows), 1)
        allowed = (sc[...] == sr[...]) & (to <= at) & (at - to < WINDOW)
        s = jnp.where(allowed, mm_t(q, k) * (hd**-0.5), -1e30)
        e = jnp.exp(s - jnp.max(s, axis=-1, keepdims=True))
        p = e / jnp.sum(e, axis=-1, keepdims=True)
        p_o[...] = p
        mix = mm(p.astype(BF), v).astype(BF)
        mix_o[...] = mix
        return mm(mix, wo[0])

    def shard(total, own, i, o):
        ng = i[5]
        residual = i[0][own].astype(F32) + rms(total) * ng[0, 1:2]
        o[8][...] = total
        o[9][...] = residual
        return [(rms(residual) * ng[0, 2:3]).astype(BF)]

    share = rows // ranks
    return call_exchange(
        [x16, w_query, w_key, w_value, w_out, norm_gains, head_gains, cos, sin, seg_col, seg_row],
        [
            struct((rows, width), BF),
            struct((rows, hd)),
            struct((rows, hd)),
            struct((rows, hd), BF),
            struct((rows, hd), BF),
            struct((rows, hd), BF),
            struct((rows, rows)),
            struct((rows, hd), BF),
            struct((share, width)),
            struct((share, width)),
        ],
        1, pre, None, shard, ranks, cid,
    )


def feed_forward(n2, residual, w, cot, ranks, cid):
    _, _, _, _, w_gate, w_up, w_down, norm_gains, _ = w
    width = n2.shape[1]
    units = w_gate.shape[-1]
    rows = MB_TOK
    share = rows // ranks

    def pre(i, o):
        n2_ref, res, wg, wu, wd, ng = i[:6]
        n2 = n2_ref[...]
        gate = mm(n2, wg[0])
        up = mm(n2, wu[0])
        h = (gelu_parts(gate)[0] * up).astype(BF)
        o[0][...] = gate
        o[1][...] = up
        o[2][...] = h
        return mm(h, wd[0])

    def shard(total, own, i, o):
        res, ng = i[1], i[5]
        gain = ng[0, 3:4]
        y16 = (res[...] + rms(total) * gain).astype(BF)
        o[3][...] = total
        if cot is None:
            return [y16]
        d_mlp, d_gain = rms_back(total, gain, i[6][own].astype(F32))
        o[4][...] = d_gain
        return [y16, d_mlp.astype(BF)]

    outs = [struct((rows, units)), struct((rows, units)), struct((rows, units), BF), struct((share, width))]
    ins = [n2, residual, w_gate, w_up, w_down, norm_gains]
    if cot is not None:
        ins.append(cot)
        outs.append(struct((1, width)))
    return call_exchange(ins, outs, 1 if cot is None else 2, pre, None, shard, ranks, cid)


def feed_backward(d_mlp16, dy16, kept, w, ranks, cid):
    _, _, _, _, w_gate, w_up, w_down, norm_gains, _ = w
    n2, gate, up, h, residual, attended = kept
    width = n2.shape[1]
    units = w_gate.shape[-1]
    rows = MB_TOK
    share = rows // ranks

    def pre(i, o):
        dm, _, _, gate, up, _, _, _, wg, wu, wd, _ = i
        dh = mm_t(dm[...], wd[0])
        value, slope = gelu_parts(gate[...])
        dg = (dh * up[...] * slope).astype(BF)
        du = (dh * value).astype(BF)
        o[4][...] = dg
        o[5][...] = du
        return mm_t(dg, wg[0]) + mm_t(du, wu[0])

    def during(i, o):
        dm, n2, h = i[0], i[2], i[5]
        o[0][:, :units] = t_mm(n2[...], o[4][...]).astype(BF)
        o[0][:, units : 2 * units] = t_mm(n2[...], o[5][...]).astype(BF)
        o[0][:, 2 * units :] = t_mm(dm[...], h[...]).astype(BF)

    def shard(total, own, i, o):
        dy, res, att, ng = i[1], i[6], i[7], i[11]
        d_branch, dg2 = rms_back(res[...], ng[0, 2:3], total)
        dr = dy[own].astype(F32) + d_branch
        d_att, dg1 = rms_back(att[...], ng[0, 1:2], dr)
        o[1][...] = dr
        o[2][...] = dg1
        o[3][...] = dg2
        return [d_att.astype(BF)]

    return call_exchange(
        [d_mlp16, dy16, n2, gate, up, h, residual, attended, w_gate, w_up, w_down, norm_gains],
        [
            struct((width, 3 * units), BF),
            struct((share, width)),
            struct((1, width)),
            struct((1, width)),
            struct((rows, units), BF),
            struct((rows, units), BF),
        ],
        1, pre, during, shard, ranks, cid,
    )


def attend_backward(d_att16, dr, x16, kept, w, tables, below, ranks, cid):
    w_query, w_key, w_value, w_out, _, _, _, norm_gains, head_gains = w
    n1, qr, kr, q, k, v, p, mix = kept
    cos, sin = tables[:2]
    width = n1.shape[1]
    hd = w_key.shape[-1]
    rows = MB_TOK

    def pre(i, o):
        da, _, _, n1, qr, kr, q, k, v, p, mix, cos, sin, wq, wk, wv, wo, _, hg = i[:19]
        scale = hd**-0.5
        do = mm_t(da[...], wo[0]).astype(BF)
        p = p[...]
        d_p = mm_t(do, v[...])
        ds = (p * (d_p - jnp.sum(p * d_p, axis=-1, keepdims=True))).astype(BF)
        dq = mm(ds, k[...]) * scale
        dk = t_mm(ds, q[...]) * scale
        dv = t_mm(p.astype(BF), do).astype(BF)
        dq_raw, dgq = rms_back(qr[...], hg[0, 0:1], rope_back(dq, cos[...], sin[...]))
        dk_raw, dgk = rms_back(kr[...], hg[0, 1:2], rope_back(dk, cos[...], sin[...]))
        dq_raw = dq_raw.astype(BF)
        dk_raw = dk_raw.astype(BF)
        o[2][...] = dgq
        o[3][...] = dgk
        o[4][...] = dq_raw
        o[5][...] = dk_raw
        o[6][...] = dv
        return mm_t(dq_raw, wq[0]) + mm_t(dk_raw, wk[0]) + mm_t(dv, wv[0])

    def during(i, o):
        da, n1, mix = i[0][...], i[3][...], i[10][...]
        o[0][:, :hd] = t_mm(n1, o[4][...]).astype(BF)
        o[0][:, hd : 2 * hd] = t_mm(da, mix).astype(BF)
        o[0][:, 2 * hd : 3 * hd] = t_mm(n1, o[5][...]).astype(BF)
        o[0][:, 3 * hd :] = t_mm(n1, o[6][...]).astype(BF)

    def shard(total, own, i, o):
        d_branch, dg0 = rms_back(i[2][own].astype(F32), i[17][0, 0:1], total)
        o[1][...] = dg0
        dx16 = (i[1][...] + d_branch).astype(BF)
        if below is None:
            return [dx16]
        d_mlp, dg3 = rms_back(i[19][...], i[20][0, 3:4], dx16.astype(F32))
        o[7][...] = dg3
        return [dx16, d_mlp.astype(BF)]

    ins = [d_att16, dr, x16, n1, qr, kr, q, k, v, p, mix, cos, sin]
    ins += [w_query, w_key, w_value, w_out, norm_gains, head_gains]
    outs = [
        struct((width, 4 * hd), BF),
        struct((1, width)),
        struct((1, hd)),
        struct((1, hd)),
        struct((rows, hd), BF),
        struct((rows, hd), BF),
        struct((rows, hd), BF),
    ]
    if below is not None:
        ins += list(below)
        outs.append(struct((1, width)))
    return call_exchange(ins, outs, 1 if below is None else 2, pre, during, shard, ranks, cid)


def reduce_kernel(nt, nd, hd, *refs):
    (ga0, ga1, gm0, gm1, s0, s1, y0, y1, x0, x1) = refs[:10]
    (out_a, out_m, out_kv, out_s, out_y, out_x) = refs[10:16]
    (swap_a, swap_m, swap_s, h_a, h_m, r_a, r_m, kv_part, kv_recv, s_sum, s_recv) = refs[16:27]
    (sw_send, sw_recv, sm_send, sm_recv, lo_sem, dp_send, dp_recv, kt_send, kt_recv) = refs[27:36]
    (ka_send, ka_recv, ss_send, ss_recv) = refs[36:]
    sec = lax.axis_index("section")
    t = lax.axis_index("tensor")
    z = lax.axis_index("dp")
    total = nt * nd
    me = z * nt + t
    rows = ga0.shape[0] // nd
    section = {"section": 1 - sec}
    group = []
    for step in range(1, total):
        flat = lax.rem(me + step, total)
        group.append({"dp": flat // nt, "tensor": lax.rem(flat, nt)})
    barrier = pltpu.get_barrier_semaphore()
    for device in [section] + group:
        pl.semaphore_signal(barrier, inc=1, device_id=device, device_id_type=MESH)
    pl.semaphore_wait(barrier, total)

    def remote(src, dst, send, recv, device):
        return pltpu.make_async_remote_copy(
            src_ref=src, dst_ref=dst, send_sem=send, recv_sem=recv,
            device_id=device, device_id_type=MESH,
        )

    zs = [lax.rem(z + d, nd) for d in range(1, nd)] + [z]
    spans = [pl.ds(pl.multiple_of(peer * rows, rows), rows) for peer in zs]

    def swap(ga, gm, s, y, x):
        first = [remote(s, swap_s, sm_send.at[0], sm_recv.at[0], section)]
        for n, span in enumerate(spans):
            first.append(remote(ga.at[span], swap_a.at[span], sw_send.at[0, n], sw_recv.at[0, n], section))
        for n, span in enumerate(spans):
            first.append(remote(gm.at[span], swap_m.at[span], sw_send.at[1, n], sw_recv.at[1, n], section))
        first.append(remote(y, out_y.at[sec], sm_send.at[1], sm_recv.at[1], section))
        first.append(remote(x, out_x.at[sec], sm_send.at[2], sm_recv.at[2], section))
        return first

    @pl.when(sec == 0)
    def _():
        for copy in swap(ga1, gm1, s1, y1, x1):
            copy.start()
        pltpu.make_async_copy(y0, out_y.at[0], lo_sem.at[0]).start()
        pltpu.make_async_copy(x0, out_x.at[0], lo_sem.at[1]).start()

    @pl.when(sec == 1)
    def _():
        for copy in swap(ga0, gm0, s0, y0, x0):
            copy.start()
        pltpu.make_async_copy(y1, out_y.at[1], lo_sem.at[0]).start()
        pltpu.make_async_copy(x1, out_x.at[1], lo_sem.at[1]).start()

    waits = swap(ga0, gm0, s0, y0, x0)
    waits[0].wait_recv()

    @pl.when(sec == 0)
    def _():
        s_sum[...] = s0[...] + swap_s[...]

    @pl.when(sec == 1)
    def _():
        s_sum[...] = s1[...] + swap_s[...]

    s_copies = []
    for step, device in enumerate(group):
        copy = remote(s_sum, s_recv.at[step], ss_send.at[step], ss_recv.at[step], device)
        copy.start()
        s_copies.append(copy)
    dp_copies = []
    for kind, (g_0, g_1, got, held, landed) in enumerate(
        ((ga0, ga1, swap_a, h_a, r_a), (gm0, gm1, swap_m, h_m, r_m))
    ):
        for n in range(nd):
            waits[1 + kind * nd + n].wait_recv()
            span = spans[n]

            @pl.when(sec == 0)
            def _():
                held[n] = (g_0[span].astype(F32) + got[span].astype(F32)).astype(BF)

            @pl.when(sec == 1)
            def _():
                held[n] = (g_1[span].astype(F32) + got[span].astype(F32)).astype(BF)

            if n < nd - 1:
                copy = remote(
                    held.at[n], landed.at[n], dp_send.at[kind, n], dp_recv.at[kind, n], {"dp": zs[n]}
                )
                copy.start()
                dp_copies.append(copy)
    for n in range(nd - 1):
        dp_copies[n].wait_recv()
    acc = h_a[nd - 1].astype(F32)
    for n in range(nd - 1):
        acc = acc + r_a[n].astype(F32)
    out_a[...] = acc[:, : 2 * hd]
    piece = 2 * hd // nt
    for n in range(nt):
        kv_part[n] = acc[:, 2 * hd + n * piece : 2 * hd + (n + 1) * piece].astype(BF)
    kt_copies = []
    for d in range(1, nt):
        peer = lax.rem(t + d, nt)
        copy = remote(
            kv_part.at[peer], kv_recv.at[d - 1], kt_send.at[d - 1], kt_recv.at[d - 1], {"tensor": peer}
        )
        copy.start()
        kt_copies.append(copy)
    mine = kv_part[t].astype(F32)
    for d, copy in enumerate(kt_copies):
        copy.wait_recv()
        mine = mine + kv_recv[d].astype(F32)
    out_kv[me] = mine.astype(BF)
    ka_copies = []
    for step, device in enumerate(group):
        copy = remote(out_kv.at[me], out_kv.at[me], ka_send.at[step], ka_recv.at[step], device)
        copy.start()
        ka_copies.append(copy)
    acc_s = s_sum[...]
    for step, copy in enumerate(s_copies):
        copy.wait_recv()
        acc_s = acc_s + s_recv[step]
    out_s[...] = acc_s
    for n in range(nd - 1):
        dp_copies[nd - 1 + n].wait_recv()
    acc_m = h_m[nd - 1].astype(F32)
    for n in range(nd - 1):
        acc_m = acc_m + r_m[n].astype(F32)
    out_m[...] = acc_m
    waits[-2].wait_recv()
    waits[-1].wait_recv()
    pltpu.make_async_copy(y0, out_y.at[sec], lo_sem.at[0]).wait()
    pltpu.make_async_copy(x0, out_x.at[sec], lo_sem.at[1]).wait()
    for copy in ka_copies:
        copy.wait()
    for copy in waits + s_copies + dp_copies + kt_copies:
        copy.wait_send()


def reduce_all(grads_a, grads_m, smalls, ys, xs, nt, nd, hd):
    width, wa = grads_a[0].shape
    wm = grads_m[0].shape[1]
    rows = width // nd
    total = nt * nd
    dma = pltpu.SemaphoreType.DMA
    ins = list(grads_a) + list(grads_m) + list(smalls) + list(ys) + list(xs)
    tok = ys[0].shape
    return pl.pallas_call(
        functools.partial(reduce_kernel, nt, nd, hd),
        out_shape=[
            struct((rows, 2 * hd)),
            struct((rows, wm)),
            struct((total, rows, 2 * hd // nt), BF),
            struct(smalls[0].shape),
            struct((2,) + tok, BF),
            struct((2,) + tok, BF),
        ],
        in_specs=[VM] * len(ins),
        out_specs=[VM] * 6,
        scratch_shapes=[
            pltpu.VMEM((width, wa), BF),
            pltpu.VMEM((width, wm), BF),
            pltpu.VMEM(smalls[0].shape, F32),
            pltpu.VMEM((nd, rows, wa), BF),
            pltpu.VMEM((nd, rows, wm), BF),
            pltpu.VMEM((nd - 1, rows, wa), BF),
            pltpu.VMEM((nd - 1, rows, wm), BF),
            pltpu.VMEM((nt, rows, 2 * hd // nt), BF),
            pltpu.VMEM((nt - 1, rows, 2 * hd // nt), BF),
            pltpu.VMEM(smalls[0].shape, F32),
            pltpu.VMEM((total - 1,) + smalls[0].shape, F32),
            dma((2, nd)), dma((2, nd)), dma((3,)), dma((3,)), dma((2,)),
            dma((2, nd - 1)), dma((2, nd - 1)), dma((nt - 1,)), dma((nt - 1,)),
            dma((total - 1,)), dma((total - 1,)), dma((total - 1,)), dma((total - 1,)),
        ],
        compiler_params=pltpu.CompilerParams(
            collective_id=2, has_side_effects=True, vmem_limit_bytes=VMEM_LIMIT
        ),
    )(*ins)


def reduce_plain(grads_a, grads_m, smalls, ys, xs, nt, nd, hd):
    sec = lax.axis_index("section")
    pairs = [(0, 1), (1, 0)]

    def own_sum(pair):
        own = jnp.where(sec == 0, pair[0], pair[1])
        other = jnp.where(sec == 0, pair[1], pair[0])
        return own.astype(F32) + lax.ppermute(other, "section", pairs).astype(F32)

    def placed(pair):
        own = jnp.where(sec == 0, pair[0], pair[1])
        other = lax.ppermute(jnp.where(sec == 0, pair[1], pair[0]), "section", pairs)
        return jnp.stack([jnp.where(sec == 0, own, other), jnp.where(sec == 0, other, own)])

    g_a, g_m, small = own_sum(grads_a), own_sum(grads_m), own_sum(smalls)
    split = jnp.concatenate([g_a[:, : 2 * hd], g_m], axis=1).astype(BF)
    split = lax.psum_scatter(split, "dp", scatter_dimension=0, tiled=True).astype(F32)
    kv, small = lax.psum((g_a[:, 2 * hd :], small), ("tensor", "dp"))
    return split[:, : 2 * hd], split[:, 2 * hd :], kv, small, placed(ys), placed(xs)


def per_device(tokens, segments, cotangent, *weights):
    nt, nd = lax.axis_size("tensor"), lax.axis_size("dp")
    sec = lax.axis_index("section")
    width = tokens.shape[1]
    hd = weights[1].shape[-1]
    units = weights[4].shape[-1]
    rows = MB_TOK
    x16 = lax.dynamic_slice_in_dim(tokens, sec * rows, rows, 0)
    cot = lax.dynamic_slice_in_dim(cotangent, sec * rows, rows, 0)
    seg = lax.dynamic_slice_in_dim(segments, sec * rows, rows, 0)
    w0, w1 = both_layers(weights)
    at = jnp.arange(rows, dtype=jnp.int32)
    seen = (seg[:, None] == seg[None, :]) & (at[None, :] <= at[:, None])
    position = (jnp.sum(seen.astype(jnp.int32), axis=1) - 1).astype(F32)
    freq = jnp.exp(jnp.arange(hd // 2, dtype=F32) * (-2.0 * math.log(10000.0) / hd))
    angles = position[:, None] * freq[None, :]
    tables = (jnp.cos(angles), jnp.sin(angles), seg[:, None], seg[None, :])

    n2_0, *kept_0, att_0, res_0 = attend_forward(x16, w0, tables, nt, 3)
    y_0, gate_0, up_0, h_0, mlp_0 = feed_forward(n2_0, res_0, w0, None, nt, 4)
    n2_1, *kept_1, att_1, res_1 = attend_forward(y_0, w1, tables, nt, 3)
    y_1, d_mlp_1, gate_1, up_1, h_1, _, dg3_1 = feed_forward(n2_1, res_1, w1, cot, nt, 5)

    d_att_1, gm_1, dr_1, dg1_1, dg2_1, _, _ = feed_backward(
        d_mlp_1, cot, (n2_1, gate_1, up_1, h_1, res_1, att_1), w1, nt, 6
    )
    dx_1, d_mlp_0, ga_1, dg0_1, dgq_1, dgk_1, _, _, _, dg3_0 = attend_backward(
        d_att_1, dr_1, y_0, kept_1, w1, tables, (mlp_0, w0[7]), nt, 7
    )
    d_att_0, gm_0, dr_0, dg1_0, dg2_0, _, _ = feed_backward(
        d_mlp_0, dx_1, (n2_0, gate_0, up_0, h_0, res_0, att_0), w0, nt, 6
    )
    dx_0, ga_0, dg0_0, dgq_0, dgk_0, _, _, _ = attend_backward(
        d_att_0, dr_0, x16, kept_0, w0, tables, None, nt, 8
    )

    def small(g0, g1, g2, g3, q, k):
        tail = ((0, 2), (0, width - hd))
        return jnp.concatenate([g0, g1, g2, g3, jnp.pad(jnp.concatenate([q, k]), tail)])

    smalls = (
        small(dg0_0, dg1_0, dg2_0, dg3_0, dgq_0, dgk_0),
        small(dg0_1, dg1_1, dg2_1, dg3_1, dgq_1, dgk_1),
    )
    fits = width % (16 * nd) == 0 and (2 * hd // nt) % 128 == 0 and nt * nd <= 32
    reducer = reduce_all if fits else reduce_plain
    g_a, g_m, kv, sums, out_y, out_x = reducer(
        (ga_0, ga_1), (gm_0, gm_1), smalls, (y_0, y_1), (dx_0, dx_1), nt, nd, hd
    )
    if fits:
        kv = kv.reshape(nd, nt, width // nd, 2 * hd // nt).transpose(0, 2, 1, 3).reshape(width, 2 * hd)
        kv = kv.astype(F32)
    cols = width // nd
    gains = lax.dynamic_slice(sums, (0, lax.axis_index("dp") * cols), (4, cols))
    return (
        out_y.astype(F32).reshape(1, 2 * rows, width),
        out_x.astype(F32).reshape(1, 2 * rows, width),
        g_a[None, :, :hd],
        kv[None, :, :hd],
        kv[None, :, hd:],
        g_a[:, hd:].T[None],
        g_m[None, :, :units],
        g_m[None, :, units : 2 * units],
        g_m[:, 2 * units :].T[None],
        gains[None],
        sums[None, 4:6, :hd],
    )


def solution(mesh):
    return jax.shard_map(
        per_device,
        mesh=mesh,
        in_specs=(
            P("dp", None),
            P("dp"),
            P("dp", None),
            P("section", None, "tensor"),
            P("section", None, None),
            P("section", None, None),
            P("section", "tensor", None),
            P("section", None, "tensor"),
            P("section", None, "tensor"),
            P("section", "tensor", None),
            P("section", None, None),
            P("section", None, None),
        ),
        out_specs=(
            P("section", "dp", None),
            P("section", "dp", None),
            P("section", "dp", "tensor"),
            P("section", None, None),
            P("section", None, None),
            P("section", "tensor", "dp"),
            P("section", "dp", "tensor"),
            P("section", "dp", "tensor"),
            P("section", "tensor", "dp"),
            P("section", None, "dp"),
            P("section", None, None),
        ),
        check_vma=False,
    )
```

time: 818 us -> 340 us (0.42)
  waiting for transfers between devices: 470 us -> 0 us
  Pallas kernels: 0 us -> 320 us
  blocking collectives: 160 us -> 0 us
  other arithmetic: 69.5 us -> 3.17 us
  matrix products: 54.4 us -> 0 us
  between operations: 18.2 us -> 1 us
  local copies, waits for them, and re-layouts: 28.7 us -> 12.1 us
    reduce_scatter x17 -> x0, waiting for transfers between devices: 327 us -> none  [the longest x3 79.3 us: forward(): lax.psum_scatter(attn_part, 'tensor', scatter_dimension=0, tiled=True)]
    pallas_call x0 -> x10, Pallas kernels: none -> 320 us  [the longest x8 121 us: call_exchange(): pl.pallas_call(kernel, out_shape=[jax.ShapeDtypeStruct((rows, width), BF)...]
    all_gather x12 -> x0, blocking collectives: 119 us -> none  [the longest x3 31.5 us: forward(): mlp_sum = lax.all_gather(mlp_piece, 'tensor', axis=0, tiled=True)]
    psum x1 -> x0, waiting for transfers between devices: 118 us -> none  [per_device(): lax.psum((g_key, g_value, head_grads), ('tensor', 'dp'))]
    dot_general x81 -> x0, matrix products: 54.4 us -> none  [the longest x21 15.3 us: dot_first(): lax.dot_general(former, latter, (((0,), (0,)), ((), ())), preferred_eleme...]
    psum x1 -> x0, blocking collectives: 41.7 us -> none  [per_device(): lax.psum((g_key, g_value, head_grads), ('tensor', 'dp'))]
    reduce_sum x36 -> x1, other arithmetic: 27.4 us -> 0.18 us  [per_device(): position = (jnp.sum(seen.astype(jnp.int32), axis=1) - 1).astype(F32)]
    unnamed x594 -> x37, local copies, waits for them, and re-layouts: 25.8 us -> 5.06 us
  transfers between devices with their start and end apart: 23 -> 0, of which waited for: 21 -> 0; matrix products, arithmetic and copies ran while one was open for 5% -> 0% of each run, Pallas kernels for 0% -> 0%
where the time goes in v1:
time: 340 us; the launch traced here: 337 us
  Pallas kernels  320 us (94%)
  local copies, waits for them, and re-layouts  12.1 us (4%)
    pallas_call x8, Pallas kernels, call_exchange(): pl.pallas_call(kernel, out_shape=[jax.ShapeDtypeStruct((rows, width), BF)...  121 us
    pallas_call x1, Pallas kernels, both_layers(): pl.pallas_call(functools.partial(swap_kernel, count), out_shape=shapes *...  101 us
    pallas_call x1, Pallas kernels, reduce_all(): pl.pallas_call(functools.partial(reduce_kernel, nt, nd, hd), out_shape=[s...  98 us

profile of v1, /device:TPU:0, one launch (start us, length us, event | category | flops | bytes accessed | tf_op | source)
XLA Modules:
  0.0 336.5 jit_solution(16213452326197656799)
XLA Ops:
  0.7 0.8 dynamic_slice.13
  1.4 0.2 convert_reduce_fusion
  1.6 0.1 copy.27.refs_9_
  1.8 0.5 multiply_sine_fusion
  2.3 1.1 constant_dynamic-slice_fusion
  3.4 101.5 %shard_map.203 = (bf16[1,640,256]{2,1,0:T(8,128)(2,1)}, bf16[1,640,256]{2,1,0:T(8,128)(2,1)}, bf16[1,640,256]{2,1,0:T(8,128)(2,1)}, bf16[1,256,640]{2,1,0:T(8,12...) custom-call(bf16[1,640,256]{2,1,0:T(8,128)(2,1)} %refs_0_.1, ...), custom_call_target="tpu_custom_call" | custom-call | tf_op jit(solution)/shard_map/pallas_call | solution.py:180
  105.0 1.1 copy-done.3
  106.0 1.0 copy-done.5
  107.0 1.0 copy-done.7
  108.0 0.7 copy-done.11
  108.7 0.7 copy-done.14
  109.4 15.8 %shard_map.204 = (bf16[256,640]{1,0:T(8,128)(2,1)S(1)}, bf16[256,640]{1,0:T(8,128)(2,1)S(1)}, f32[256,256]{1,0:T(8,128)S(1)}, f32[256,256]{1,0:T(8,128)S(1)}, bf...) custom-call(bf16[256,640]{1,0:T(8,128)(2,1)S(1)} %get-tuple-element., ...), custom_call_target="tpu_custom_call" | custom-call | tf_op jit(solution)/shard_map/pallas_call | solution.py:128
  125.1 0.0 copy-start.8
  125.2 12.6 %shard_map.205 = (bf16[256,640]{1,0:T(8,128)(2,1)S(1)}, f32[256,512]{1,0:T(8,128)S(1)}, f32[256,512]{1,0:T(8,128)S(1)}, bf16[256,512]{1,0:T(8,128)(2,1)S(1)}, f32[64,640]{1,0:T(8,128)S(1)}) custom-call(bf16[256,640]{1,0:T(8,128)(2,1)S(1)} %get-tuple-element.96.refs_0_.refs_2_, f32[64,640]{1,0:T(8,128)S(1)} %get-tuple-element.97.refs_1_.refs_6_, ...), custom_call_target="tpu_custom_call" | custom-call | tf_op jit(solution)/shard_map/pallas_call | solution.py:128
  137.8 13.2 %shard_map.206 = (bf16[256,640]{1,0:T(8,128)(2,1)S(1)}, bf16[256,640]{1,0:T(8,128)(2,1)S(1)}, f32[256,256]{1,0:T(8,128)S(1)}, f32[256,256]{1,0:T(8,128)S(1)}, bf...) custom-call(bf16[256,640]{1,0:T(8,128)(2,1)S(1)} %get-tuple-element., ...), custom_call_target="tpu_custom_call" | custom-call | tf_op jit(solution)/shard_map/pallas_call | solution.py:128
  151.0 17.3 %shard_map.207 = (bf16[256,640]{1,0:T(8,128)(2,1)S(1)}, bf16[256,640]{1,0:T(8,128)(2,1)S(1)}, f32[256,512]{1,0:T(8,128)S(1)}, f32[256,512]{1,0:T(8,128)S(1)}, bf...) custom-call(bf16[256,640]{1,0:T(8,128)(2,1)S(1)} %get-tuple-element.108.refs_0_.refs_2_, ...), custom_call_target="tpu_custom_call" | custom-call | tf_op jit(solution)/shard_map/pallas_call | solution.py:128
  168.4 15.4 %shard_map.208 = (bf16[256,640]{1,0:T(8,128)(2,1)S(1)}, bf16[640,1536]{1,0:T(8,128)(2,1)}, f32[64,640]{1,0:T(8,128)S(1)}, f32[1,640]{1,0:T(1,128)S(1)}, f32[1,64...) custom-call(bf16[256,640]{1,0:T(8,128)(2,1)S(1)} %get-tuple-element.113.refs_0_, ...), custom_call_target="tpu_custom_call" | custom-call | tf_op jit(solution)/shard_map/pallas_call | solution.py:128
  183.8 17.6 %shard_map.209 = (bf16[256,640]{1,0:T(8,128)(2,1)S(1)}, bf16[256,640]{1,0:T(8,128)(2,1)S(1)}, bf16[640,1024]{1,0:T(8,128)(2,1)}, f32[1,640]{1,0:T(1,128)S(1)}, f...) custom-call(bf16[256,640]{1,0:T(8,128)(2,1)S(1)} %get-tuple-element., ...), custom_call_target="tpu_custom_call" | custom-call | tf_op jit(solution)/shard_map/pallas_call | solution.py:128
  201.4 14.4 %shard_map.210 = (bf16[256,640]{1,0:T(8,128)(2,1)S(1)}, bf16[640,1536]{1,0:T(8,128)(2,1)}, f32[64,640]{1,0:T(8,128)S(1)}, f32[1,640]{1,0:T(1,128)S(1)}, f32[1,64...) custom-call(bf16[256,640]{1,0:T(8,128)(2,1)S(1)} %get-tuple-element.129.refs_0_, ...), custom_call_target="tpu_custom_call" | custom-call | tf_op jit(solution)/shard_map/pallas_call | solution.py:128
  215.8 14.6 %shard_map.211 = (bf16[256,640]{1,0:T(8,128)(2,1)S(1)}, bf16[640,1024]{1,0:T(8,128)(2,1)}, f32[1,640]{1,0:T(1,128)S(1)}, f32[1,256]{1,0:T(1,128)S(1)}, f32[1,256...) custom-call(bf16[256,640]{1,0:T(8,128)(2,1)S(1)} %get-tuple-element.135.refs_0_, ...), custom_call_target="tpu_custom_call" | custom-call | tf_op jit(solution)/shard_map/pallas_call | solution.py:128
  230.5 98.0 %shard_map.212 = (f32[160,512]{1,0:T(8,128)S(1)}, f32[160,1536]{1,0:T(8,128)}, bf16[16,160,128]{2,1,0:T(8,128)(2,1)S(1)}, f32[8,640]{1,0:T(8,128)S(1)}, bf16[2,2...) custom-call(bf16[640,1024]{1,0:T(8,128)(2,1)} %get-tuple-element.145.refs_0_, ...), custom_call_target="tpu_custom_call" | custom-call | tf_op jit(solution)/shard_map/pallas_call | solution.py:551
  328.5 0.6 slice_bitcast_fusion.7
  329.1 0.7 dynamic-slice_bitcast_fusion
  329.8 0.7 slice_bitcast_fusion.5
  330.5 1.1 bitcast_convert_fusion
  331.7 1.1 bitcast_convert_fusion.1
  332.8 0.5 copy-done.17
  333.3 1.0 slice_bitcast_fusion.2
  334.3 0.1 convert_bitcast_fusion
  334.4 0.8 copy.29
  335.3 0.1 copy.32
  335.4 1.2 slice_bitcast_fusion
  (35 shorter events, 0.2 us)
Async XLA Ops:
  104.9 20.2 %copy-start = (bf16[1,640,512]{2,1,0:T(8,128)(2,1)S(1)}, bf16[1,640,512]{2,1,0:T(8,128)(2,1)}, u32[]{:S(2)}) copy-start(bf16[1,640,512]{2,1,0:T(8,128)(2,1)} %get-tuple-element.98.refs_2_.refs_8_) | copy-start | bytes 1966084
  104.9 20.2 %copy-start.1 = (bf16[1,640,512]{2,1,0:T(8,128)(2,1)S(1)}, bf16[1,640,512]{2,1,0:T(8,128)(2,1)}, u32[]{:S(2)}) copy-start(bf16[1,640,512]{2,1,0:T(8,128)(2,1)} %get-tuple-element.99.refs_3_.refs_9_) | copy-start | bytes 1966084
  104.9 1.1 copy-start.3
  106.0 1.0 copy-start.5
  107.0 1.0 copy-start.7
  108.0 0.7 copy-start.11
  108.7 0.7 copy-start.14
  125.1 12.7 %copy-start.8 = (bf16[1,640,256]{2,1,0:T(8,128)(2,1)S(1)}, bf16[1,640,256]{2,1,0:T(8,128)(2,1)}, u32[]{:S(2)}) copy-start(bf16[1,640,256]{2,1,0:T(8,128)(2,1)} %get-tuple-element.102.refs_1_.refs_13_) | copy-start | bytes 983044
  125.1 12.7 %copy-start.9 = (bf16[1,640,256]{2,1,0:T(8,128)(2,1)S(1)}, bf16[1,640,256]{2,1,0:T(8,128)(2,1)}, u32[]{:S(2)}) copy-start(bf16[1,640,256]{2,1,0:T(8,128)(2,1)} %get-tuple-element.103.refs_2_.refs_14_) | copy-start | bytes 983044
  125.1 12.7 %copy-start.10 = (bf16[1,640,256]{2,1,0:T(8,128)(2,1)S(1)}, bf16[1,640,256]{2,1,0:T(8,128)(2,1)}, u32[]{:S(2)}) copy-start(bf16[1,640,256]{2,1,0:T(8,128)(2,1)} %get-tuple-element.104.refs_3_.refs_15_) | copy-start | bytes 983044
  125.2 12.7 %copy-start.13 = (f32[1,4,640]{2,1,0:T(4,128)S(1)}, f32[1,4,640]{2,1,0:T(4,128)}, u32[]{:S(2)}) copy-start(f32[1,4,640]{2,1,0:T(4,128)} %get-tuple-element.106.refs_5_.refs_11_.refs_17_) | copy-start | bytes 30724
  125.2 12.7 %copy-start.16 = (f32[1,2,256]{2,1,0:T(2,128)S(1)}, f32[1,2,256]{2,1,0:T(2,128)}, u32[]{:S(2)}) copy-start(f32[1,2,256]{2,1,0:T(2,128)} %get-tuple-element.107.refs_6_.refs_18_) | copy-start | bytes 6148
  137.8 13.3 %copy-start.2 = (bf16[1,640,512]{2,1,0:T(8,128)(2,1)S(1)}, bf16[1,640,512]{2,1,0:T(8,128)(2,1)}, u32[]{:S(2)}) copy-start(bf16[1,640,512]{2,1,0:T(8,128)(2,1)} %get-tuple-element.110.refs_2_.refs_8_) | copy-start | bytes 1966084
  168.4 15.4 %copy-start.12 = (f32[1,4,640]{2,1,0:T(4,128)S(1)}, f32[1,4,640]{2,1,0:T(4,128)}, u32[]{:S(2)}) copy-start(f32[1,4,640]{2,1,0:T(4,128)} %get-tuple-element.94.refs_5_.refs_20_.refs_11_.refs_17_) | copy-start | bytes 30724
  201.4 14.4 %copy-start.4 = (bf16[1,640,256]{2,1,0:T(8,128)(2,1)S(1)}, bf16[1,640,256]{2,1,0:T(8,128)(2,1)}, u32[]{:S(2)}) copy-start(bf16[1,640,256]{2,1,0:T(8,128)(2,1)} %get-tuple-element.90.refs_1_.refs_13_) | copy-start | bytes 983044
  201.4 14.4 %copy-start.6 = (bf16[1,640,256]{2,1,0:T(8,128)(2,1)S(1)}, bf16[1,640,256]{2,1,0:T(8,128)(2,1)}, u32[]{:S(2)}) copy-start(bf16[1,640,256]{2,1,0:T(8,128)(2,1)} %get-tuple-element.91.refs_2_.refs_14_) | copy-start | bytes 983044
  201.4 14.4 %copy-start.15 = (f32[1,2,256]{2,1,0:T(2,128)S(1)}, f32[1,2,256]{2,1,0:T(2,128)}, u32[]{:S(2)}) copy-start(f32[1,2,256]{2,1,0:T(2,128)} %get-tuple-element.95.refs_6_.refs_18_) | copy-start | bytes 6148
  331.7 1.7 copy-start.17

commit v2 on v1

--- a/solution.py
+++ b/solution.py
@@ -15,7 +15,6 @@
 F32 = jnp.float32
 MESH = pl.DeviceIdType.MESH
 VM = pl.BlockSpec(memory_space=pltpu.VMEM)
-ANY = pl.BlockSpec(memory_space=pl.ANY)
 VMEM_LIMIT = 50 * 1024 * 1024
 
 
@@ -180,10 +179,12 @@
     outs = pl.pallas_call(
         functools.partial(swap_kernel, count),
         out_shape=shapes * 2,
-        in_specs=[ANY] * count,
-        out_specs=[ANY] * (2 * count),
+        in_specs=[VM] * count,
+        out_specs=[VM] * (2 * count),
         scratch_shapes=[pltpu.SemaphoreType.DMA((count,))] * 3,
-        compiler_params=pltpu.CompilerParams(collective_id=1, has_side_effects=True),
+        compiler_params=pltpu.CompilerParams(
+            collective_id=1, has_side_effects=True, vmem_limit_bytes=VMEM_LIMIT
+        ),
     )(*weights)
     return outs[:count], outs[count:]
 

time: 340 us -> 245 us (0.72)
  Pallas kernels: 320 us -> 229 us
    pallas_call x1, Pallas kernels: 101 us -> 9.59 us  [both_layers(): pl.pallas_call(functools.partial(swap_kernel, count), out_shape=shapes *...]
where the time goes in v2:
time: 245 us; the launch traced here: 242 us
  Pallas kernels  229 us (93%)
  local copies, waits for them, and re-layouts  9.26 us (4%)
  other arithmetic  3.17 us (1%)
    pallas_call x8, Pallas kernels, call_exchange(): pl.pallas_call(kernel, out_shape=[jax.ShapeDtypeStruct((rows, width), BF)...  120 us
    pallas_call x1, Pallas kernels, reduce_all(): pl.pallas_call(functools.partial(reduce_kernel, nt, nd, hd), out_shape=[s...  98.7 us
    pallas_call x1, Pallas kernels, both_layers(): pl.pallas_call(functools.partial(swap_kernel, count), out_shape=shapes *...  9.59 us

profile of v2, /device:TPU:0, one launch (start us, length us, event | category | flops | bytes accessed | tf_op | source)
XLA Modules:
  0.0 242.0 jit_solution(635908966805922677)
XLA Ops:
  0.6 0.0 copy-start.14
  0.7 0.0 copy-start.13
  0.7 0.0 copy-start.12
  0.7 0.9 dynamic_slice.13
  1.6 0.2 convert_reduce_fusion
  1.8 0.1 copy.27.refs_9_
  1.9 0.5 multiply_sine_fusion
  2.5 1.1 constant_dynamic-slice_fusion
  3.7 9.6 %shard_map.203 = (bf16[1,640,256]{2,1,0:T(8,128)(2,1)S(1)}, bf16[1,640,256]{2,1,0:T(8,128)(2,1)S(1)}, bf16[1,640,256]{2,1,0:T(8,128)(2,1)S(1)}, bf16[1,256,640]{...) custom-call(bf16[1,640,256]{2,1,0:T(8,128)(2,1)S(1)} %copy-done.9, ...), custom_call_target="tpu_custom_call" | custom-call | tf_op jit(solution)/shard_map/pallas_call | solution.py:179
  13.3 0.0 copy-start.4
  13.3 0.7 copy-done.4
  14.0 0.7 copy-done.8
  14.7 16.2 %shard_map.204 = (bf16[256,640]{1,0:T(8,128)(2,1)S(1)}, bf16[256,640]{1,0:T(8,128)(2,1)S(1)}, f32[256,256]{1,0:T(8,128)S(1)}, f32[256,256]{1,0:T(8,128)S(1)}, bf...) custom-call(bf16[256,640]{1,0:T(8,128)(2,1)S(1)} %get-tuple-element., ...), custom_call_target="tpu_custom_call" | custom-call | tf_op jit(solution)/shard_map/pallas_call | solution.py:127
  31.0 12.4 %shard_map.205 = (bf16[256,640]{1,0:T(8,128)(2,1)S(1)}, f32[256,512]{1,0:T(8,128)S(1)}, f32[256,512]{1,0:T(8,128)S(1)}, bf16[256,512]{1,0:T(8,128)(2,1)S(1)}, f32[64,640]{1,0:T(8,128)S(1)}) custom-call(bf16[256,640]{1,0:T(8,128)(2,1)S(1)} %get-tuple-element.96.refs_0_.refs_2_, f32[64,640]{1,0:T(8,128)S(1)} %get-tuple-element.97.refs_1_.refs_6_, ...), custom_call_target="tpu_custom_call" | custom-call | tf_op jit(solution)/shard_map/pallas_call | solution.py:127
  43.4 13.4 %shard_map.206 = (bf16[256,640]{1,0:T(8,128)(2,1)S(1)}, bf16[256,640]{1,0:T(8,128)(2,1)S(1)}, f32[256,256]{1,0:T(8,128)S(1)}, f32[256,256]{1,0:T(8,128)S(1)}, bf...) custom-call(bf16[256,640]{1,0:T(8,128)(2,1)S(1)} %get-tuple-element., ...), custom_call_target="tpu_custom_call" | custom-call | tf_op jit(solution)/shard_map/pallas_call | solution.py:127
  56.8 16.8 %shard_map.207 = (bf16[256,640]{1,0:T(8,128)(2,1)S(1)}, bf16[256,640]{1,0:T(8,128)(2,1)S(1)}, f32[256,512]{1,0:T(8,128)S(1)}, f32[256,512]{1,0:T(8,128)S(1)}, bf...) custom-call(bf16[256,640]{1,0:T(8,128)(2,1)S(1)} %get-tuple-element.108.refs_0_.refs_2_, ...), custom_call_target="tpu_custom_call" | custom-call | tf_op jit(solution)/shard_map/pallas_call | solution.py:127
  73.7 15.3 %shard_map.208 = (bf16[256,640]{1,0:T(8,128)(2,1)S(1)}, bf16[640,1536]{1,0:T(8,128)(2,1)}, f32[64,640]{1,0:T(8,128)S(1)}, f32[1,640]{1,0:T(1,128)S(1)}, f32[1,64...) custom-call(bf16[256,640]{1,0:T(8,128)(2,1)S(1)} %get-tuple-element.113.refs_0_, ...), custom_call_target="tpu_custom_call" | custom-call | tf_op jit(solution)/shard_map/pallas_call | solution.py:127
  89.0 17.1 %shard_map.209 = (bf16[256,640]{1,0:T(8,128)(2,1)S(1)}, bf16[256,640]{1,0:T(8,128)(2,1)S(1)}, bf16[640,1024]{1,0:T(8,128)(2,1)}, f32[1,640]{1,0:T(1,128)S(1)}, f...) custom-call(bf16[256,640]{1,0:T(8,128)(2,1)S(1)} %get-tuple-element., ...), custom_call_target="tpu_custom_call" | custom-call | tf_op jit(solution)/shard_map/pallas_call | solution.py:127
  106.1 15.8 %shard_map.210 = (bf16[256,640]{1,0:T(8,128)(2,1)S(1)}, bf16[640,1536]{1,0:T(8,128)(2,1)}, f32[64,640]{1,0:T(8,128)S(1)}, f32[1,640]{1,0:T(1,128)S(1)}, f32[1,64...) custom-call(bf16[256,640]{1,0:T(8,128)(2,1)S(1)} %get-tuple-element.129.refs_0_, ...), custom_call_target="tpu_custom_call" | custom-call | tf_op jit(solution)/shard_map/pallas_call | solution.py:127
  122.0 13.2 %shard_map.211 = (bf16[256,640]{1,0:T(8,128)(2,1)S(1)}, bf16[640,1024]{1,0:T(8,128)(2,1)}, f32[1,640]{1,0:T(1,128)S(1)}, f32[1,256]{1,0:T(1,128)S(1)}, f32[1,256...) custom-call(bf16[256,640]{1,0:T(8,128)(2,1)S(1)} %get-tuple-element.135.refs_0_, ...), custom_call_target="tpu_custom_call" | custom-call | tf_op jit(solution)/shard_map/pallas_call | solution.py:127
  135.3 98.7 %shard_map.212 = (f32[160,512]{1,0:T(8,128)S(1)}, f32[160,1536]{1,0:T(8,128)}, bf16[16,160,128]{2,1,0:T(8,128)(2,1)S(1)}, f32[8,640]{1,0:T(8,128)S(1)}, bf16[2,2...) custom-call(bf16[640,1024]{1,0:T(8,128)(2,1)} %get-tuple-element.145.refs_0_, ...), custom_call_target="tpu_custom_call" | custom-call | tf_op jit(solution)/shard_map/pallas_call | solution.py:552
  234.0 0.6 slice_bitcast_fusion.7
  234.6 0.7 dynamic-slice_bitcast_fusion
  235.3 0.7 slice_bitcast_fusion.5
  236.0 1.1 bitcast_convert_fusion
  237.1 1.1 bitcast_convert_fusion.1
  238.3 0.5 copy-done.15
  238.8 1.0 slice_bitcast_fusion.2
  239.8 0.1 convert_bitcast_fusion
  239.9 0.8 copy.29
  240.8 0.1 copy.32
  240.9 1.2 slice_bitcast_fusion
  (31 shorter events, 0.2 us)
Async XLA Ops:
  0.6 3.0 %copy-start.14 = (f32[1,2,256]{2,1,0:T(2,128)S(1)}, f32[1,2,256]{2,1,0:T(2,128)}, u32[]{:S(2)}) copy-start(f32[1,2,256]{2,1,0:T(2,128)} %refs_8_.1) | copy-start | bytes 6148
  0.7 3.0 %copy-start.13 = (f32[1,4,640]{2,1,0:T(4,128)S(1)}, f32[1,4,640]{2,1,0:T(4,128)}, u32[]{:S(2)}) copy-start(f32[1,4,640]{2,1,0:T(4,128)} %refs_7_.1) | copy-start | bytes 30724
  0.7 3.0 %copy-start.12 = (bf16[1,256,640]{2,1,0:T(8,128)(2,1)S(1)}, bf16[1,256,640]{2,1,0:T(8,128)(2,1)}, u32[]{:S(2)}) copy-start(bf16[1,256,640]{2,1,0:T(8,128)(2,1)} %refs_3_.1) | copy-start | bytes 983044
  0.7 3.0 %copy-start.11 = (bf16[1,640,256]{2,1,0:T(8,128)(2,1)S(1)}, bf16[1,640,256]{2,1,0:T(8,128)(2,1)}, u32[]{:S(2)}) copy-start(bf16[1,640,256]{2,1,0:T(8,128)(2,1)} %refs_2_.1) | copy-start | bytes 983044
  0.7 3.0 %copy-start.10 = (bf16[1,640,256]{2,1,0:T(8,128)(2,1)S(1)}, bf16[1,640,256]{2,1,0:T(8,128)(2,1)}, u32[]{:S(2)}) copy-start(bf16[1,640,256]{2,1,0:T(8,128)(2,1)} %refs_1_.1) | copy-start | bytes 983044
  0.7 3.0 %copy-start.9 = (bf16[1,640,256]{2,1,0:T(8,128)(2,1)S(1)}, bf16[1,640,256]{2,1,0:T(8,128)(2,1)}, u32[]{:S(2)}) copy-start(bf16[1,640,256]{2,1,0:T(8,128)(2,1)} %refs_0_.1) | copy-start | bytes 983044
  13.3 0.7 copy-start.4
  14.0 0.7 copy-start.8
  14.7 28.7 %copy-start.3 = (bf16[1,640,256]{2,1,0:T(8,128)(2,1)}, bf16[1,640,256]{2,1,0:T(8,128)(2,1)S(1)}, u32[]{:S(2)}) copy-start(bf16[1,640,256]{2,1,0:T(8,128)(2,1)S(1)} %get-tuple-element.92.refs_3_.refs_15_) | copy-start | bytes 983044
  14.7 28.7 %copy-start.5 = (bf16[1,640,256]{2,1,0:T(8,128)(2,1)}, bf16[1,640,256]{2,1,0:T(8,128)(2,1)S(1)}, u32[]{:S(2)}) copy-start(bf16[1,640,256]{2,1,0:T(8,128)(2,1)S(1)} %get-tuple-element.102.refs_1_.refs_13_) | copy-start | bytes 983044
  14.7 28.7 %copy-start.6 = (bf16[1,640,256]{2,1,0:T(8,128)(2,1)}, bf16[1,640,256]{2,1,0:T(8,128)(2,1)S(1)}, u32[]{:S(2)}) copy-start(bf16[1,640,256]{2,1,0:T(8,128)(2,1)S(1)} %get-tuple-element.103.refs_2_.refs_14_) | copy-start | bytes 983044
  14.7 28.7 %copy-start.7 = (bf16[1,640,256]{2,1,0:T(8,128)(2,1)}, bf16[1,640,256]{2,1,0:T(8,128)(2,1)S(1)}, u32[]{:S(2)}) copy-start(bf16[1,640,256]{2,1,0:T(8,128)(2,1)S(1)} %get-tuple-element.104.refs_3_.refs_15_) | copy-start | bytes 983044
  14.7 16.2 %copy-start = (bf16[1,640,512]{2,1,0:T(8,128)(2,1)S(1)}, bf16[1,640,512]{2,1,0:T(8,128)(2,1)}, u32[]{:S(2)}) copy-start(bf16[1,640,512]{2,1,0:T(8,128)(2,1)} %get-tuple-element.98.refs_2_.refs_8_) | copy-start | bytes 1966084
  14.7 16.2 %copy-start.1 = (bf16[1,640,512]{2,1,0:T(8,128)(2,1)S(1)}, bf16[1,640,512]{2,1,0:T(8,128)(2,1)}, u32[]{:S(2)}) copy-start(bf16[1,640,512]{2,1,0:T(8,128)(2,1)} %get-tuple-element.99.refs_3_.refs_9_) | copy-start | bytes 1966084
  43.4 13.4 %copy-start.2 = (bf16[1,640,512]{2,1,0:T(8,128)(2,1)S(1)}, bf16[1,640,512]{2,1,0:T(8,128)(2,1)}, u32[]{:S(2)}) copy-start(bf16[1,640,512]{2,1,0:T(8,128)(2,1)} %get-tuple-element.110.refs_2_.refs_8_) | copy-start | bytes 1966084
  237.1 1.7 copy-start.15

commit v3 on v2

--- a/solution.py
+++ b/solution.py
@@ -68,7 +68,86 @@
     return value, slope
 
 
-def call_exchange(ins, out_shapes, gathered, pre, during, shard, ranks, collective_id):
+class GradSum:
+    def __init__(self, nd, grad):
+        self.nd = nd
+        self.half = grad.shape[0] // (2 * nd)
+        self.width = grad.shape[1]
+
+    def scratch(self):
+        dma = pltpu.SemaphoreType.DMA
+        block = (self.half, self.width)
+        return [
+            pltpu.VMEM((self.nd,) + block, BF),
+            pltpu.VMEM((self.nd,) + block, BF),
+            pltpu.VMEM((self.nd - 1,) + block, BF),
+            dma((self.nd,)), dma((self.nd,)), dma((self.nd - 1,)), dma((self.nd - 1,)),
+        ]
+
+    def result(self):
+        return struct((self.half, self.width))
+
+    def devices(self):
+        z = lax.axis_index("dp")
+        peers = [{"dp": lax.rem(z + d, self.nd)} for d in range(1, self.nd)]
+        return [{"section": 1 - lax.axis_index("section")}] + peers
+
+    def begin(self, grad, refs):
+        self.grad = grad
+        self.got, self.held, self.landed, sw_send, sw_recv, self.dp_send, self.dp_recv = refs
+        sec, z = lax.axis_index("section"), lax.axis_index("dp")
+        self.zs = [lax.rem(z + d, self.nd) for d in range(1, self.nd)] + [z]
+        self.swaps = []
+        for n, peer in enumerate(self.zs):
+            copy = pltpu.make_async_remote_copy(
+                src_ref=grad.at[self.rows(peer, 1 - sec)],
+                dst_ref=self.got.at[n],
+                send_sem=sw_send.at[n],
+                recv_sem=sw_recv.at[n],
+                device_id={"section": 1 - sec},
+                device_id_type=MESH,
+            )
+            copy.start()
+            self.swaps.append(copy)
+
+    def rows(self, peer, core):
+        return pl.ds(pl.multiple_of((2 * peer + core) * self.half, self.half), self.half)
+
+    def send(self):
+        sec = lax.axis_index("section")
+        self.sends = []
+        for n, peer in enumerate(self.zs):
+            self.swaps[n].wait_recv()
+            own = self.grad[self.rows(peer, sec)].astype(F32)
+            self.held[n] = (own + self.got[n].astype(F32)).astype(BF)
+            if n < self.nd - 1:
+                copy = pltpu.make_async_remote_copy(
+                    src_ref=self.held.at[n],
+                    dst_ref=self.landed.at[n],
+                    send_sem=self.dp_send.at[n],
+                    recv_sem=self.dp_recv.at[n],
+                    device_id={"dp": peer},
+                    device_id_type=MESH,
+                )
+                copy.start()
+                self.sends.append(copy)
+
+    def finish(self):
+        total = self.held[self.nd - 1].astype(F32)
+        for n, copy in enumerate(self.sends):
+            copy.wait_recv()
+            total = total + self.landed[n].astype(F32)
+        for copy in self.swaps + self.sends:
+            copy.wait_send()
+        return total
+
+
+def call_exchange(ins, out_shapes, gathered, pre, during, shard, ranks, collective_id, behind=None):
+    job = None
+    if behind is not None:
+        job = GradSum(lax.axis_size("dp"), behind)
+        ins = ins + [behind]
+        out_shapes = out_shapes + [job.result()]
     n_in, n_out = len(ins), len(out_shapes)
     rows, width = MB_TOK, ins[0].shape[-1]
     share = rows // ranks
@@ -77,15 +156,21 @@
         in_refs = refs[:n_in]
         gat = refs[n_in : n_in + gathered]
         outs = refs[n_in + gathered : n_in + gathered + n_out]
-        part, recv, rs_send, rs_recv, ag_send, ag_recv = refs[n_in + gathered + n_out :]
+        scratch = refs[n_in + gathered + n_out :]
+        part, recv, rs_send, rs_recv, ag_send, ag_recv = scratch[:6]
         me = lax.axis_index("tensor")
         peers = [lax.rem(me + d, ranks) for d in range(1, ranks)]
         barrier = pltpu.get_barrier_semaphore()
-        for peer in peers:
-            pl.semaphore_signal(barrier, inc=1, device_id={"tensor": peer}, device_id_type=MESH)
+        devices = [{"tensor": peer} for peer in peers] + (job.devices() if job else [])
+        for device in devices:
+            pl.semaphore_signal(barrier, inc=1, device_id=device, device_id_type=MESH)
         own = pl.ds(pl.multiple_of(me * share, share), share)
+        if job:
+            pl.semaphore_wait(barrier, len(devices))
+            job.begin(in_refs[-1], scratch[6:])
         part[...] = pre(in_refs, outs).astype(BF)
-        pl.semaphore_wait(barrier, ranks - 1)
+        if not job:
+            pl.semaphore_wait(barrier, len(devices))
         copies = []
         for d, peer in enumerate(peers):
             copy = pltpu.make_async_remote_copy(
@@ -98,6 +183,8 @@
             )
             copy.start()
             copies.append(copy)
+        if job:
+            job.send()
         if during is not None:
             during(in_refs, outs)
         total = part[own].astype(F32)
@@ -123,6 +210,8 @@
             copy.wait_send()
         for copy in sends:
             copy.wait()
+        if job:
+            outs[-1][...] = job.finish()
 
     return pl.pallas_call(
         kernel,
@@ -136,7 +225,8 @@
             pltpu.SemaphoreType.DMA((ranks - 1,)),
             pltpu.SemaphoreType.DMA((gathered, ranks - 1)),
             pltpu.SemaphoreType.DMA((gathered, ranks - 1)),
-        ],
+        ]
+        + (job.scratch() if job else []),
         compiler_params=pltpu.CompilerParams(
             collective_id=collective_id, has_side_effects=True, vmem_limit_bytes=VMEM_LIMIT
         ),
@@ -289,7 +379,7 @@
     return call_exchange(ins, outs, 1 if cot is None else 2, pre, None, shard, ranks, cid)
 
 
-def feed_backward(d_mlp16, dy16, kept, w, ranks, cid):
+def feed_backward(d_mlp16, dy16, kept, w, ranks, cid, behind=None):
     _, _, _, _, w_gate, w_up, w_down, norm_gains, _ = w
     n2, gate, up, h, residual, attended = kept
     width = n2.shape[1]
@@ -298,7 +388,7 @@
     share = rows // ranks
 
     def pre(i, o):
-        dm, _, _, gate, up, _, _, _, wg, wu, wd, _ = i
+        dm, _, _, gate, up, _, _, _, wg, wu, wd, _ = i[:12]
         dh = mm_t(dm[...], wd[0])
         value, slope = gelu_parts(gate[...])
         dg = (dh * up[...] * slope).astype(BF)
@@ -333,11 +423,11 @@
             struct((rows, units), BF),
             struct((rows, units), BF),
         ],
-        1, pre, during, shard, ranks, cid,
-    )
-
-
-def attend_backward(d_att16, dr, x16, kept, w, tables, below, ranks, cid):
+        1, pre, during, shard, ranks, cid, behind,
+    )
+
+
+def attend_backward(d_att16, dr, x16, kept, w, tables, below, ranks, cid, behind=None):
     w_query, w_key, w_value, w_out, _, _, _, norm_gains, head_gains = w
     n1, qr, kr, q, k, v, p, mix = kept
     cos, sin = tables[:2]
@@ -397,21 +487,19 @@
     if below is not None:
         ins += list(below)
         outs.append(struct((1, width)))
-    return call_exchange(ins, outs, 1 if below is None else 2, pre, during, shard, ranks, cid)
-
-
-def reduce_kernel(nt, nd, hd, *refs):
-    (ga0, ga1, gm0, gm1, s0, s1, y0, y1, x0, x1) = refs[:10]
+    return call_exchange(ins, outs, 1 if below is None else 2, pre, during, shard, ranks, cid, behind)
+
+
+def reduce_kernel(job, nt, nd, hd, *refs):
+    (ga0, ra1, rm0, rm1, s0, s1, y0, y1, x0, x1) = refs[:10]
     (out_a, out_m, out_kv, out_s, out_y, out_x) = refs[10:16]
-    (swap_a, swap_m, swap_s, h_a, h_m, r_a, r_m, kv_part, kv_recv, s_sum, s_recv) = refs[16:27]
-    (sw_send, sw_recv, sm_send, sm_recv, lo_sem, dp_send, dp_recv, kt_send, kt_recv) = refs[27:36]
-    (ka_send, ka_recv, ss_send, ss_recv) = refs[36:]
+    (swap_s, ra0, both_a, kv_part, kv_recv, s_sum, s_recv) = refs[16:23]
+    (sm_send, sm_recv, lo_sem, kt_send, kt_recv, ka_send, ka_recv, ss_send, ss_recv) = refs[23:32]
     sec = lax.axis_index("section")
     t = lax.axis_index("tensor")
     z = lax.axis_index("dp")
     total = nt * nd
     me = z * nt + t
-    rows = ga0.shape[0] // nd
     section = {"section": 1 - sec}
     group = []
     for step in range(1, total):
@@ -428,34 +516,37 @@
             device_id=device, device_id_type=MESH,
         )
 
-    zs = [lax.rem(z + d, nd) for d in range(1, nd)] + [z]
-    spans = [pl.ds(pl.multiple_of(peer * rows, rows), rows) for peer in zs]
-
-    def swap(ga, gm, s, y, x):
-        first = [remote(s, swap_s, sm_send.at[0], sm_recv.at[0], section)]
-        for n, span in enumerate(spans):
-            first.append(remote(ga.at[span], swap_a.at[span], sw_send.at[0, n], sw_recv.at[0, n], section))
-        for n, span in enumerate(spans):
-            first.append(remote(gm.at[span], swap_m.at[span], sw_send.at[1, n], sw_recv.at[1, n], section))
-        first.append(remote(y, out_y.at[sec], sm_send.at[1], sm_recv.at[1], section))
-        first.append(remote(x, out_x.at[sec], sm_send.at[2], sm_recv.at[2], section))
-        return first
+    mine_rows = pl.ds(pl.multiple_of(sec * job.half, job.half), job.half)
+
+    def swap(s, m, y, x):
+        return [
+            remote(s, swap_s, sm_send.at[0], sm_recv.at[0], section),
+            remote(m, out_m.at[mine_rows], sm_send.at[1], sm_recv.at[1], section),
+            remote(y, out_y.at[sec], sm_send.at[2], sm_recv.at[2], section),
+            remote(x, out_x.at[sec], sm_send.at[3], sm_recv.at[3], section),
+        ]
+
+    def keep(m, y, x):
+        return [
+            pltpu.make_async_copy(m, out_m.at[mine_rows], lo_sem.at[0]),
+            pltpu.make_async_copy(y, out_y.at[sec], lo_sem.at[1]),
+            pltpu.make_async_copy(x, out_x.at[sec], lo_sem.at[2]),
+        ]
+
+    job.begin(ga0, refs[32:])
 
     @pl.when(sec == 0)
     def _():
-        for copy in swap(ga1, gm1, s1, y1, x1):
+        for copy in swap(s1, rm1, y1, x1) + keep(rm0, y0, x0):
             copy.start()
-        pltpu.make_async_copy(y0, out_y.at[0], lo_sem.at[0]).start()
-        pltpu.make_async_copy(x0, out_x.at[0], lo_sem.at[1]).start()
 
     @pl.when(sec == 1)
     def _():
-        for copy in swap(ga0, gm0, s0, y0, x0):
+        for copy in swap(s0, rm0, y0, x0) + keep(rm1, y1, x1):
             copy.start()
-        pltpu.make_async_copy(y1, out_y.at[1], lo_sem.at[0]).start()
-        pltpu.make_async_copy(x1, out_x.at[1], lo_sem.at[1]).start()
-
-    waits = swap(ga0, gm0, s0, y0, x0)
+
+    job.send()
+    waits = swap(s0, rm0, y0, x0)
     waits[0].wait_recv()
 
     @pl.when(sec == 0)
@@ -471,37 +562,27 @@
         copy = remote(s_sum, s_recv.at[step], ss_send.at[step], ss_recv.at[step], device)
         copy.start()
         s_copies.append(copy)
-    dp_copies = []
-    for kind, (g_0, g_1, got, held, landed) in enumerate(
-        ((ga0, ga1, swap_a, h_a, r_a), (gm0, gm1, swap_m, h_m, r_m))
-    ):
-        for n in range(nd):
-            waits[1 + kind * nd + n].wait_recv()
-            span = spans[n]
-
-            @pl.when(sec == 0)
-            def _():
-                held[n] = (g_0[span].astype(F32) + got[span].astype(F32)).astype(BF)
-
-            @pl.when(sec == 1)
-            def _():
-                held[n] = (g_1[span].astype(F32) + got[span].astype(F32)).astype(BF)
-
-            if n < nd - 1:
-                copy = remote(
-                    held.at[n], landed.at[n], dp_send.at[kind, n], dp_recv.at[kind, n], {"dp": zs[n]}
-                )
-                copy.start()
-                dp_copies.append(copy)
-    for n in range(nd - 1):
-        dp_copies[n].wait_recv()
-    acc = h_a[nd - 1].astype(F32)
-    for n in range(nd - 1):
-        acc = acc + r_a[n].astype(F32)
-    out_a[...] = acc[:, : 2 * hd]
+    ra0[...] = job.finish()
+
+    def swap_a(a):
+        return remote(a, both_a.at[mine_rows], sm_send.at[4], sm_recv.at[4], section)
+
+    @pl.when(sec == 0)
+    def _():
+        swap_a(ra1).start()
+        both_a[mine_rows] = ra0[...]
+
+    @pl.when(sec == 1)
+    def _():
+        swap_a(ra0).start()
+        both_a[mine_rows] = ra1[...]
+
+    waits.append(swap_a(ra0))
+    waits[4].wait_recv()
+    out_a[...] = both_a[:, : 2 * hd]
     piece = 2 * hd // nt
     for n in range(nt):
-        kv_part[n] = acc[:, 2 * hd + n * piece : 2 * hd + (n + 1) * piece].astype(BF)
+        kv_part[n] = both_a[:, 2 * hd + n * piece : 2 * hd + (n + 1) * piece].astype(BF)
     kt_copies = []
     for d in range(1, nt):
         peer = lax.rem(t + d, nt)
@@ -525,32 +606,26 @@
         copy.wait_recv()
         acc_s = acc_s + s_recv[step]
     out_s[...] = acc_s
-    for n in range(nd - 1):
-        dp_copies[nd - 1 + n].wait_recv()
-    acc_m = h_m[nd - 1].astype(F32)
-    for n in range(nd - 1):
-        acc_m = acc_m + r_m[n].astype(F32)
-    out_m[...] = acc_m
-    waits[-2].wait_recv()
-    waits[-1].wait_recv()
-    pltpu.make_async_copy(y0, out_y.at[sec], lo_sem.at[0]).wait()
-    pltpu.make_async_copy(x0, out_x.at[sec], lo_sem.at[1]).wait()
+    for copy in waits[1:4]:
+        copy.wait_recv()
+    for copy in keep(rm0, y0, x0):
+        copy.wait()
     for copy in ka_copies:
         copy.wait()
-    for copy in waits + s_copies + dp_copies + kt_copies:
+    for copy in waits + s_copies + kt_copies:
         copy.wait_send()
 
 
 def reduce_all(grads_a, grads_m, smalls, ys, xs, nt, nd, hd):
-    width, wa = grads_a[0].shape
-    wm = grads_m[0].shape[1]
-    rows = width // nd
+    job = GradSum(nd, grads_a[0])
+    wa, wm = grads_a[0].shape[1], grads_m[0].shape[1]
+    rows = 2 * job.half
     total = nt * nd
     dma = pltpu.SemaphoreType.DMA
     ins = list(grads_a) + list(grads_m) + list(smalls) + list(ys) + list(xs)
     tok = ys[0].shape
     return pl.pallas_call(
-        functools.partial(reduce_kernel, nt, nd, hd),
+        functools.partial(reduce_kernel, job, nt, nd, hd),
         out_shape=[
             struct((rows, 2 * hd)),
             struct((rows, wm)),
@@ -562,21 +637,17 @@
         in_specs=[VM] * len(ins),
         out_specs=[VM] * 6,
         scratch_shapes=[
-            pltpu.VMEM((width, wa), BF),
-            pltpu.VMEM((width, wm), BF),
             pltpu.VMEM(smalls[0].shape, F32),
-            pltpu.VMEM((nd, rows, wa), BF),
-            pltpu.VMEM((nd, rows, wm), BF),
-            pltpu.VMEM((nd - 1, rows, wa), BF),
-            pltpu.VMEM((nd - 1, rows, wm), BF),
+            pltpu.VMEM((job.half, wa), F32),
+            pltpu.VMEM((rows, wa), F32),
             pltpu.VMEM((nt, rows, 2 * hd // nt), BF),
             pltpu.VMEM((nt - 1, rows, 2 * hd // nt), BF),
             pltpu.VMEM(smalls[0].shape, F32),
             pltpu.VMEM((total - 1,) + smalls[0].shape, F32),
-            dma((2, nd)), dma((2, nd)), dma((3,)), dma((3,)), dma((2,)),
-            dma((2, nd - 1)), dma((2, nd - 1)), dma((nt - 1,)), dma((nt - 1,)),
+            dma((5,)), dma((5,)), dma((3,)), dma((nt - 1,)), dma((nt - 1,)),
             dma((total - 1,)), dma((total - 1,)), dma((total - 1,)), dma((total - 1,)),
-        ],
+        ]
+        + job.scratch(),
         compiler_params=pltpu.CompilerParams(
             collective_id=2, has_side_effects=True, vmem_limit_bytes=VMEM_LIMIT
         ),
@@ -630,15 +701,18 @@
     d_att_1, gm_1, dr_1, dg1_1, dg2_1, _, _ = feed_backward(
         d_mlp_1, cot, (n2_1, gate_1, up_1, h_1, res_1, att_1), w1, nt, 6
     )
-    dx_1, d_mlp_0, ga_1, dg0_1, dgq_1, dgk_1, _, _, _, dg3_0 = attend_backward(
-        d_att_1, dr_1, y_0, kept_1, w1, tables, (mlp_0, w0[7]), nt, 7
-    )
-    d_att_0, gm_0, dr_0, dg1_0, dg2_0, _, _ = feed_backward(
-        d_mlp_0, dx_1, (n2_0, gate_0, up_0, h_0, res_0, att_0), w0, nt, 6
-    )
-    dx_0, ga_0, dg0_0, dgq_0, dgk_0, _, _, _ = attend_backward(
-        d_att_0, dr_0, x16, kept_0, w0, tables, None, nt, 8
-    )
+    fits = width % (32 * nd) == 0 and (2 * hd // nt) % 128 == 0 and nt * nd <= 32
+    dx_1, d_mlp_0, ga_1, dg0_1, dgq_1, dgk_1, _, _, _, dg3_0, *sum_m1 = attend_backward(
+        d_att_1, dr_1, y_0, kept_1, w1, tables, (mlp_0, w0[7]), nt, 7, gm_1 if fits else None
+    )
+    d_att_0, gm_0, dr_0, dg1_0, dg2_0, _, _, *sum_a1 = feed_backward(
+        d_mlp_0, dx_1, (n2_0, gate_0, up_0, h_0, res_0, att_0), w0, nt, 9, ga_1 if fits else None
+    )
+    dx_0, ga_0, dg0_0, dgq_0, dgk_0, _, _, _, *sum_m0 = attend_backward(
+        d_att_0, dr_0, x16, kept_0, w0, tables, None, nt, 8, gm_0 if fits else None
+    )
+    if fits:
+        ga_1, gm_0, gm_1 = sum_a1[0], sum_m0[0], sum_m1[0]
 
     def small(g0, g1, g2, g3, q, k):
         tail = ((0, 2), (0, width - hd))
@@ -648,7 +722,6 @@
         small(dg0_0, dg1_0, dg2_0, dg3_0, dgq_0, dgk_0),
         small(dg0_1, dg1_1, dg2_1, dg3_1, dgq_1, dgk_1),
     )
-    fits = width % (16 * nd) == 0 and (2 * hd // nt) % 128 == 0 and nt * nd <= 32
     reducer = reduce_all if fits else reduce_plain
     g_a, g_m, kv, sums, out_y, out_x = reducer(
         (ga_0, ga_1), (gm_0, gm_1), smalls, (y_0, y_1), (dx_0, dx_1), nt, nd, hd

time: 245 us -> 228 us (0.931)
  Pallas kernels: 229 us -> 208 us
    pallas_call x1, Pallas kernels: 98.7 us -> 46 us  [reduce_all(): pl.pallas_call(functools.partial(reduce_kernel, job, nt, nd, hd), out_sha...]
    pallas_call x8, Pallas kernels: 120 us -> 153 us  [call_exchange(): pl.pallas_call(kernel, out_shape=[jax.ShapeDtypeStruct((rows, width), BF)...]
where the time goes in v3:
time: 228 us; the launch traced here: 224 us
  Pallas kernels  208 us (91%)
  local copies, waits for them, and re-layouts  10.3 us (5%)
  other arithmetic  4.25 us (2%)
    pallas_call x8, Pallas kernels, call_exchange(): pl.pallas_call(kernel, out_shape=[jax.ShapeDtypeStruct((rows, width), BF)...  153 us
    pallas_call x1, Pallas kernels, reduce_all(): pl.pallas_call(functools.partial(reduce_kernel, job, nt, nd, hd), out_sha...  46 us
    pallas_call x1, Pallas kernels, both_layers(): pl.pallas_call(functools.partial(swap_kernel, count), out_shape=shapes *...  9.64 us

profile of v3, /device:TPU:0, one launch (start us, length us, event | category | flops | bytes accessed | tf_op | source)
XLA Modules:
  0.0 224.0 jit_solution(7843374588018597415)
XLA Ops:
  0.6 0.0 copy-start.16
  0.7 0.0 copy-start.15
  0.7 0.9 dynamic_slice.13
  1.6 0.2 convert_reduce_fusion
  1.8 0.1 copy.27.refs_9_
  1.9 0.5 multiply_sine_fusion
  2.5 1.1 constant_dynamic-slice_fusion
  3.7 9.6 %shard_map.203 = (bf16[1,640,256]{2,1,0:T(8,128)(2,1)S(1)}, bf16[1,640,256]{2,1,0:T(8,128)(2,1)S(1)}, bf16[1,640,256]{2,1,0:T(8,128)(2,1)S(1)}, bf16[1,256,640]{...) custom-call(bf16[1,640,256]{2,1,0:T(8,128)(2,1)S(1)} %copy-done.11, ...), custom_call_target="tpu_custom_call" | custom-call | tf_op jit(solution)/shard_map/pallas_call | solution.py:269
  13.3 0.0 copy-start.4
  13.3 0.7 copy-done.4
  14.0 0.7 copy-done.8
  14.8 16.2 %shard_map.204 = (bf16[256,640]{1,0:T(8,128)(2,1)S(1)}, bf16[256,640]{1,0:T(8,128)(2,1)S(1)}, f32[256,256]{1,0:T(8,128)S(1)}, f32[256,256]{1,0:T(8,128)S(1)}, bf...) custom-call(bf16[256,640]{1,0:T(8,128)(2,1)S(1)} %get-tuple-element., ...), custom_call_target="tpu_custom_call" | custom-call | tf_op jit(solution)/shard_map/pallas_call | solution.py:216
  31.0 12.4 %shard_map.205 = (bf16[256,640]{1,0:T(8,128)(2,1)S(1)}, f32[256,512]{1,0:T(8,128)S(1)}, f32[256,512]{1,0:T(8,128)S(1)}, bf16[256,512]{1,0:T(8,128)(2,1)S(1)}, f32[64,640]{1,0:T(8,128)S(1)}) custom-call(bf16[256,640]{1,0:T(8,128)(2,1)S(1)} %get-tuple-element.99.refs_0_.refs_2_, f32[64,640]{1,0:T(8,128)S(1)} %get-tuple-element.100.refs_1_.refs_6_, ...), custom_call_target="tpu_custom_call" | custom-call | tf_op jit(solution)/shard_map/pallas_call | solution.py:216
  43.5 13.3 %shard_map.206 = (bf16[256,640]{1,0:T(8,128)(2,1)S(1)}, bf16[256,640]{1,0:T(8,128)(2,1)S(1)}, f32[256,256]{1,0:T(8,128)S(1)}, f32[256,256]{1,0:T(8,128)S(1)}, bf...) custom-call(bf16[256,640]{1,0:T(8,128)(2,1)S(1)} %get-tuple-element., ...), custom_call_target="tpu_custom_call" | custom-call | tf_op jit(solution)/shard_map/pallas_call | solution.py:216
  56.8 16.9 %shard_map.207 = (bf16[256,640]{1,0:T(8,128)(2,1)S(1)}, bf16[256,640]{1,0:T(8,128)(2,1)S(1)}, f32[256,512]{1,0:T(8,128)S(1)}, f32[256,512]{1,0:T(8,128)S(1)}, bf...) custom-call(bf16[256,640]{1,0:T(8,128)(2,1)S(1)} %get-tuple-element.111.refs_0_.refs_2_, ...), custom_call_target="tpu_custom_call" | custom-call | tf_op jit(solution)/shard_map/pallas_call | solution.py:216
  73.7 13.8 %shard_map.208 = (bf16[256,640]{1,0:T(8,128)(2,1)S(1)}, bf16[640,1536]{1,0:T(8,128)(2,1)}, f32[64,640]{1,0:T(8,128)S(1)}, f32[1,640]{1,0:T(1,128)S(1)}, f32[1,64...) custom-call(bf16[256,640]{1,0:T(8,128)(2,1)S(1)} %get-tuple-element.116.refs_0_, ...), custom_call_target="tpu_custom_call" | custom-call | tf_op jit(solution)/shard_map/pallas_call | solution.py:216
  87.5 27.0 %shard_map.209 = (bf16[256,640]{1,0:T(8,128)(2,1)S(1)}, bf16[256,640]{1,0:T(8,128)(2,1)S(1)}, bf16[640,1024]{1,0:T(8,128)(2,1)}, f32[1,640]{1,0:T(1,128)S(1)}, f...) custom-call(bf16[256,640]{1,0:T(8,128)(2,1)S(1)} %get-tuple-element., ...), custom_call_target="tpu_custom_call" | custom-call | tf_op jit(solution)/shard_map/pallas_call | solution.py:216
  114.6 24.8 %shard_map.210 = (bf16[256,640]{1,0:T(8,128)(2,1)S(1)}, bf16[640,1536]{1,0:T(8,128)(2,1)}, f32[64,640]{1,0:T(8,128)S(1)}, f32[1,640]{1,0:T(1,128)S(1)}, f32[1,64...) custom-call(bf16[256,640]{1,0:T(8,128)(2,1)S(1)} %get-tuple-element.133.refs_0_, ...), custom_call_target="tpu_custom_call" | custom-call | tf_op jit(solution)/shard_map/pallas_call | solution.py:216
  139.4 28.3 %shard_map.211 = (bf16[256,640]{1,0:T(8,128)(2,1)S(1)}, bf16[640,1024]{1,0:T(8,128)(2,1)}, f32[1,640]{1,0:T(1,128)S(1)}, f32[1,256]{1,0:T(1,128)S(1)}, f32[1,256...) custom-call(bf16[256,640]{1,0:T(8,128)(2,1)S(1)} %get-tuple-element., ...), custom_call_target="tpu_custom_call" | custom-call | tf_op jit(solution)/shard_map/pallas_call | solution.py:216
  167.8 1.0 copy-done.10
  168.9 46.0 %shard_map.212 = (f32[160,512]{1,0:T(8,128)S(1)}, f32[160,1536]{1,0:T(8,128)}, bf16[16,160,128]{2,1,0:T(8,128)(2,1)S(1)}, f32[8,640]{1,0:T(8,128)S(1)}, bf16[2,2...) custom-call(bf16[640,1024]{1,0:T(8,128)(2,1)} %get-tuple-element.151.refs_0_, ...), custom_call_target="tpu_custom_call" | custom-call | tf_op jit(solution)/shard_map/pallas_call | solution.py:627
  214.9 0.6 slice_bitcast_fusion.7
  215.5 0.7 dynamic-slice_bitcast_fusion
  216.1 0.7 slice_bitcast_fusion.5
  216.9 2.2 bitcast_convert_fusion
  219.1 1.1 bitcast_convert_fusion.1
  220.3 0.5 copy-done.17
  220.8 1.0 slice_bitcast_fusion.2
  221.7 0.1 convert_bitcast_fusion
  221.9 0.8 copy.29
  222.7 0.1 copy.32
  222.8 1.2 slice_bitcast_fusion
  (37 shorter events, 0.2 us)
Async XLA Ops:
  0.6 3.0 %copy-start.16 = (f32[1,2,256]{2,1,0:T(2,128)S(1)}, f32[1,2,256]{2,1,0:T(2,128)}, u32[]{:S(2)}) copy-start(f32[1,2,256]{2,1,0:T(2,128)} %refs_8_.1) | copy-start | bytes 6148
  0.7 3.0 %copy-start.15 = (f32[1,4,640]{2,1,0:T(4,128)S(1)}, f32[1,4,640]{2,1,0:T(4,128)}, u32[]{:S(2)}) copy-start(f32[1,4,640]{2,1,0:T(4,128)} %refs_7_.1) | copy-start | bytes 30724
  0.7 3.0 %copy-start.14 = (bf16[1,256,640]{2,1,0:T(8,128)(2,1)S(1)}, bf16[1,256,640]{2,1,0:T(8,128)(2,1)}, u32[]{:S(2)}) copy-start(bf16[1,256,640]{2,1,0:T(8,128)(2,1)} %refs_3_.1) | copy-start | bytes 983044
  0.7 3.0 %copy-start.13 = (bf16[1,640,256]{2,1,0:T(8,128)(2,1)S(1)}, bf16[1,640,256]{2,1,0:T(8,128)(2,1)}, u32[]{:S(2)}) copy-start(bf16[1,640,256]{2,1,0:T(8,128)(2,1)} %refs_2_.1) | copy-start | bytes 983044
  0.7 3.0 %copy-start.12 = (bf16[1,640,256]{2,1,0:T(8,128)(2,1)S(1)}, bf16[1,640,256]{2,1,0:T(8,128)(2,1)}, u32[]{:S(2)}) copy-start(bf16[1,640,256]{2,1,0:T(8,128)(2,1)} %refs_1_.1) | copy-start | bytes 983044
  0.7 3.0 %copy-start.11 = (bf16[1,640,256]{2,1,0:T(8,128)(2,1)S(1)}, bf16[1,640,256]{2,1,0:T(8,128)(2,1)}, u32[]{:S(2)}) copy-start(bf16[1,640,256]{2,1,0:T(8,128)(2,1)} %refs_0_.1) | copy-start | bytes 983044
  13.3 0.7 copy-start.4
  14.0 0.7 copy-start.8
  14.8 28.7 %copy-start.3 = (bf16[1,640,256]{2,1,0:T(8,128)(2,1)}, bf16[1,640,256]{2,1,0:T(8,128)(2,1)S(1)}, u32[]{:S(2)}) copy-start(bf16[1,640,256]{2,1,0:T(8,128)(2,1)S(1)} %get-tuple-element.95.refs_3_.refs_15_) | copy-start | bytes 983044
  14.8 28.7 %copy-start.5 = (bf16[1,640,256]{2,1,0:T(8,128)(2,1)}, bf16[1,640,256]{2,1,0:T(8,128)(2,1)S(1)}, u32[]{:S(2)}) copy-start(bf16[1,640,256]{2,1,0:T(8,128)(2,1)S(1)} %get-tuple-element.105.refs_1_.refs_13_) | copy-start | bytes 983044
  14.8 28.7 %copy-start.6 = (bf16[1,640,256]{2,1,0:T(8,128)(2,1)}, bf16[1,640,256]{2,1,0:T(8,128)(2,1)S(1)}, u32[]{:S(2)}) copy-start(bf16[1,640,256]{2,1,0:T(8,128)(2,1)S(1)} %get-tuple-element.106.refs_2_.refs_14_) | copy-start | bytes 983044
  14.8 28.7 %copy-start.7 = (bf16[1,640,256]{2,1,0:T(8,128)(2,1)}, bf16[1,640,256]{2,1,0:T(8,128)(2,1)S(1)}, u32[]{:S(2)}) copy-start(bf16[1,640,256]{2,1,0:T(8,128)(2,1)S(1)} %get-tuple-element.107.refs_3_.refs_15_) | copy-start | bytes 983044
  14.8 16.2 %copy-start = (bf16[1,640,512]{2,1,0:T(8,128)(2,1)S(1)}, bf16[1,640,512]{2,1,0:T(8,128)(2,1)}, u32[]{:S(2)}) copy-start(bf16[1,640,512]{2,1,0:T(8,128)(2,1)} %get-tuple-element.101.refs_2_.refs_8_) | copy-start | bytes 1966084
  14.8 16.2 %copy-start.1 = (bf16[1,640,512]{2,1,0:T(8,128)(2,1)S(1)}, bf16[1,640,512]{2,1,0:T(8,128)(2,1)}, u32[]{:S(2)}) copy-start(bf16[1,640,512]{2,1,0:T(8,128)(2,1)} %get-tuple-element.102.refs_3_.refs_9_) | copy-start | bytes 1966084
  43.4 13.4 %copy-start.2 = (bf16[1,640,512]{2,1,0:T(8,128)(2,1)S(1)}, bf16[1,640,512]{2,1,0:T(8,128)(2,1)}, u32[]{:S(2)}) copy-start(bf16[1,640,512]{2,1,0:T(8,128)(2,1)} %get-tuple-element.113.refs_2_.refs_8_) | copy-start | bytes 1966084
  139.4 28.5 %copy-start.9 = (f32[80,1536]{1,0:T(8,128)S(1)}, f32[80,1536]{1,0:T(8,128)}, u32[]{:S(2)}) copy-start(f32[80,1536]{1,0:T(8,128)} %get-tuple-element.154.refs_3_) | copy-start | bytes 1474564
  167.8 1.0 copy-start.10
  216.1 3.0 %copy-start.18 = (bf16[2,256,640]{2,1,0:T(8,128)(2,1)S(1)}, bf16[2,256,640]{2,1,0:T(8,128)(2,1)}, u32[]{:S(2)}) copy-start(bf16[2,256,640]{2,1,0:T(8,128)(2,1)} %get-tuple-element.169) | copy-start | bytes 1966084
  219.1 1.7 copy-start.17

commit v4 on v3

--- a/solution.py
+++ b/solution.py
@@ -501,14 +501,13 @@
     total = nt * nd
     me = z * nt + t
     section = {"section": 1 - sec}
-    group = []
-    for step in range(1, total):
-        flat = lax.rem(me + step, total)
-        group.append({"dp": flat // nt, "tensor": lax.rem(flat, nt)})
+    across = [{"dp": lax.rem(z + d, nd)} for d in range(1, nd)]
+    within = [{"tensor": lax.rem(t + d, nt)} for d in range(1, nt)]
+    group = across + within
     barrier = pltpu.get_barrier_semaphore()
     for device in [section] + group:
         pl.semaphore_signal(barrier, inc=1, device_id=device, device_id_type=MESH)
-    pl.semaphore_wait(barrier, total)
+    pl.semaphore_wait(barrier, 1 + len(group))
 
     def remote(src, dst, send, recv, device):
         return pltpu.make_async_remote_copy(
@@ -558,7 +557,7 @@
         s_sum[...] = s1[...] + swap_s[...]
 
     s_copies = []
-    for step, device in enumerate(group):
+    for step, device in enumerate(across):
         copy = remote(s_sum, s_recv.at[step], ss_send.at[step], ss_recv.at[step], device)
         copy.start()
         s_copies.append(copy)
@@ -597,7 +596,7 @@
         mine = mine + kv_recv[d].astype(F32)
     out_kv[me] = mine.astype(BF)
     ka_copies = []
-    for step, device in enumerate(group):
+    for step, device in enumerate(across):
         copy = remote(out_kv.at[me], out_kv.at[me], ka_send.at[step], ka_recv.at[step], device)
         copy.start()
         ka_copies.append(copy)
@@ -606,13 +605,33 @@
         copy.wait_recv()
         acc_s = acc_s + s_recv[step]
     out_s[...] = acc_s
+    late = []
+    for d, device in enumerate(within):
+        step = nd - 1 + d
+        copy = remote(out_s, s_recv.at[step], ss_send.at[step], ss_recv.at[step], device)
+        copy.start()
+        late.append(copy)
+    step = nd - 1
+    for back in range(nd):
+        row = lax.rem(z + nd - back, nd) * nt + t
+        if back > 0:
+            ka_copies[back - 1].wait_recv()
+        for device in within:
+            copy = remote(out_kv.at[row], out_kv.at[row], ka_send.at[step], ka_recv.at[step], device)
+            copy.start()
+            late.append(copy)
+            step += 1
+    for d in range(nt - 1):
+        late[d].wait()
+        acc_s = acc_s + s_recv[nd - 1 + d]
+    out_s[...] = acc_s
     for copy in waits[1:4]:
         copy.wait_recv()
     for copy in keep(rm0, y0, x0):
         copy.wait()
-    for copy in ka_copies:
+    for copy in late[nt - 1 :]:
         copy.wait()
-    for copy in waits + s_copies + kt_copies:
+    for copy in waits + s_copies + kt_copies + ka_copies:
         copy.wait_send()
 
 

time: 228 us -> 223 us (0.978); the launches traced: 224 us -> 222 us
  no operation moved by 1% of the time
where the time goes in v4:
time: 223 us; the launch traced here: 222 us
  Pallas kernels  207 us (93%)
  local copies, waits for them, and re-layouts  10.3 us (5%)
  other arithmetic  4.25 us (2%)
    pallas_call x8, Pallas kernels, call_exchange(): pl.pallas_call(kernel, out_shape=[jax.ShapeDtypeStruct((rows, width), BF)...  153 us
    pallas_call x1, Pallas kernels, reduce_all(): pl.pallas_call(functools.partial(reduce_kernel, job, nt, nd, hd), out_sha...  44.3 us
    pallas_call x1, Pallas kernels, both_layers(): pl.pallas_call(functools.partial(swap_kernel, count), out_shape=shapes *...  9.64 us

profile of v4, /device:TPU:0, one launch (start us, length us, event | category | flops | bytes accessed | tf_op | source)
XLA Modules:
  0.0 222.2 jit_solution(90087595037582715)
XLA Ops:
  0.6 0.0 copy-start.16
  0.7 0.0 copy-start.15
  0.7 0.9 dynamic_slice.13
  1.6 0.2 convert_reduce_fusion
  1.8 0.1 copy.27.refs_9_
  1.9 0.5 multiply_sine_fusion
  2.5 1.1 constant_dynamic-slice_fusion
  3.7 9.6 %shard_map.203 = (bf16[1,640,256]{2,1,0:T(8,128)(2,1)S(1)}, bf16[1,640,256]{2,1,0:T(8,128)(2,1)S(1)}, bf16[1,640,256]{2,1,0:T(8,128)(2,1)S(1)}, bf16[1,256,640]{...) custom-call(bf16[1,640,256]{2,1,0:T(8,128)(2,1)S(1)} %copy-done.11, ...), custom_call_target="tpu_custom_call" | custom-call | tf_op jit(solution)/shard_map/pallas_call | solution.py:269
  13.3 0.0 copy-start.4
  13.3 0.7 copy-done.4
  14.0 0.7 copy-done.8
  14.8 16.2 %shard_map.204 = (bf16[256,640]{1,0:T(8,128)(2,1)S(1)}, bf16[256,640]{1,0:T(8,128)(2,1)S(1)}, f32[256,256]{1,0:T(8,128)S(1)}, f32[256,256]{1,0:T(8,128)S(1)}, bf...) custom-call(bf16[256,640]{1,0:T(8,128)(2,1)S(1)} %get-tuple-element., ...), custom_call_target="tpu_custom_call" | custom-call | tf_op jit(solution)/shard_map/pallas_call | solution.py:216
  31.0 12.4 %shard_map.205 = (bf16[256,640]{1,0:T(8,128)(2,1)S(1)}, f32[256,512]{1,0:T(8,128)S(1)}, f32[256,512]{1,0:T(8,128)S(1)}, bf16[256,512]{1,0:T(8,128)(2,1)S(1)}, f32[64,640]{1,0:T(8,128)S(1)}) custom-call(bf16[256,640]{1,0:T(8,128)(2,1)S(1)} %get-tuple-element.99.refs_0_.refs_2_, f32[64,640]{1,0:T(8,128)S(1)} %get-tuple-element.100.refs_1_.refs_6_, ...), custom_call_target="tpu_custom_call" | custom-call | tf_op jit(solution)/shard_map/pallas_call | solution.py:216
  43.5 13.3 %shard_map.206 = (bf16[256,640]{1,0:T(8,128)(2,1)S(1)}, bf16[256,640]{1,0:T(8,128)(2,1)S(1)}, f32[256,256]{1,0:T(8,128)S(1)}, f32[256,256]{1,0:T(8,128)S(1)}, bf...) custom-call(bf16[256,640]{1,0:T(8,128)(2,1)S(1)} %get-tuple-element., ...), custom_call_target="tpu_custom_call" | custom-call | tf_op jit(solution)/shard_map/pallas_call | solution.py:216
  56.8 16.9 %shard_map.207 = (bf16[256,640]{1,0:T(8,128)(2,1)S(1)}, bf16[256,640]{1,0:T(8,128)(2,1)S(1)}, f32[256,512]{1,0:T(8,128)S(1)}, f32[256,512]{1,0:T(8,128)S(1)}, bf...) custom-call(bf16[256,640]{1,0:T(8,128)(2,1)S(1)} %get-tuple-element.111.refs_0_.refs_2_, ...), custom_call_target="tpu_custom_call" | custom-call | tf_op jit(solution)/shard_map/pallas_call | solution.py:216
  73.7 13.8 %shard_map.208 = (bf16[256,640]{1,0:T(8,128)(2,1)S(1)}, bf16[640,1536]{1,0:T(8,128)(2,1)}, f32[64,640]{1,0:T(8,128)S(1)}, f32[1,640]{1,0:T(1,128)S(1)}, f32[1,64...) custom-call(bf16[256,640]{1,0:T(8,128)(2,1)S(1)} %get-tuple-element.116.refs_0_, ...), custom_call_target="tpu_custom_call" | custom-call | tf_op jit(solution)/shard_map/pallas_call | solution.py:216
  87.5 27.0 %shard_map.209 = (bf16[256,640]{1,0:T(8,128)(2,1)S(1)}, bf16[256,640]{1,0:T(8,128)(2,1)S(1)}, bf16[640,1024]{1,0:T(8,128)(2,1)}, f32[1,640]{1,0:T(1,128)S(1)}, f...) custom-call(bf16[256,640]{1,0:T(8,128)(2,1)S(1)} %get-tuple-element., ...), custom_call_target="tpu_custom_call" | custom-call | tf_op jit(solution)/shard_map/pallas_call | solution.py:216
  114.6 24.8 %shard_map.210 = (bf16[256,640]{1,0:T(8,128)(2,1)S(1)}, bf16[640,1536]{1,0:T(8,128)(2,1)}, f32[64,640]{1,0:T(8,128)S(1)}, f32[1,640]{1,0:T(1,128)S(1)}, f32[1,64...) custom-call(bf16[256,640]{1,0:T(8,128)(2,1)S(1)} %get-tuple-element.133.refs_0_, ...), custom_call_target="tpu_custom_call" | custom-call | tf_op jit(solution)/shard_map/pallas_call | solution.py:216
  139.4 28.3 %shard_map.211 = (bf16[256,640]{1,0:T(8,128)(2,1)S(1)}, bf16[640,1024]{1,0:T(8,128)(2,1)}, f32[1,640]{1,0:T(1,128)S(1)}, f32[1,256]{1,0:T(1,128)S(1)}, f32[1,256...) custom-call(bf16[256,640]{1,0:T(8,128)(2,1)S(1)} %get-tuple-element., ...), custom_call_target="tpu_custom_call" | custom-call | tf_op jit(solution)/shard_map/pallas_call | solution.py:216
  167.8 1.0 copy-done.10
  168.9 44.3 %shard_map.212 = (f32[160,512]{1,0:T(8,128)S(1)}, f32[160,1536]{1,0:T(8,128)}, bf16[16,160,128]{2,1,0:T(8,128)(2,1)S(1)}, f32[8,640]{1,0:T(8,128)S(1)}, bf16[2,2...) custom-call(bf16[640,1024]{1,0:T(8,128)(2,1)} %get-tuple-element.151.refs_0_, ...), custom_call_target="tpu_custom_call" | custom-call | tf_op jit(solution)/shard_map/pallas_call | solution.py:646
  213.1 0.6 slice_bitcast_fusion.7
  213.7 0.7 dynamic-slice_bitcast_fusion
  214.4 0.7 slice_bitcast_fusion.5
  215.1 2.2 %bitcast_convert_fusion = f32[1,512,640]{2,1,0:T(8,128)} fusion(bf16[1,512,640]{2,1,0:T(8,128)(2,1)} %bitcast.48), kind=kLoop, calls=%fused_computation.4 | loop fusion | flops 327680 | bytes 1966080 | tf_op jit(solution)/shard_map/reshape | solution.py:755
  217.3 1.1 bitcast_convert_fusion.1
  218.5 0.5 copy-done.17
  219.0 1.0 slice_bitcast_fusion.2
  220.0 0.1 convert_bitcast_fusion
  220.1 0.8 copy.29
  221.0 0.1 copy.32
  221.1 1.2 slice_bitcast_fusion
  (37 shorter events, 0.2 us)
Async XLA Ops:
  0.6 3.0 %copy-start.16 = (f32[1,2,256]{2,1,0:T(2,128)S(1)}, f32[1,2,256]{2,1,0:T(2,128)}, u32[]{:S(2)}) copy-start(f32[1,2,256]{2,1,0:T(2,128)} %refs_8_.1) | copy-start | bytes 6148
  0.7 3.0 %copy-start.15 = (f32[1,4,640]{2,1,0:T(4,128)S(1)}, f32[1,4,640]{2,1,0:T(4,128)}, u32[]{:S(2)}) copy-start(f32[1,4,640]{2,1,0:T(4,128)} %refs_7_.1) | copy-start | bytes 30724
  0.7 3.0 %copy-start.14 = (bf16[1,256,640]{2,1,0:T(8,128)(2,1)S(1)}, bf16[1,256,640]{2,1,0:T(8,128)(2,1)}, u32[]{:S(2)}) copy-start(bf16[1,256,640]{2,1,0:T(8,128)(2,1)} %refs_3_.1) | copy-start | bytes 983044
  0.7 3.0 %copy-start.13 = (bf16[1,640,256]{2,1,0:T(8,128)(2,1)S(1)}, bf16[1,640,256]{2,1,0:T(8,128)(2,1)}, u32[]{:S(2)}) copy-start(bf16[1,640,256]{2,1,0:T(8,128)(2,1)} %refs_2_.1) | copy-start | bytes 983044
  0.7 3.0 %copy-start.12 = (bf16[1,640,256]{2,1,0:T(8,128)(2,1)S(1)}, bf16[1,640,256]{2,1,0:T(8,128)(2,1)}, u32[]{:S(2)}) copy-start(bf16[1,640,256]{2,1,0:T(8,128)(2,1)} %refs_1_.1) | copy-start | bytes 983044
  0.7 3.0 %copy-start.11 = (bf16[1,640,256]{2,1,0:T(8,128)(2,1)S(1)}, bf16[1,640,256]{2,1,0:T(8,128)(2,1)}, u32[]{:S(2)}) copy-start(bf16[1,640,256]{2,1,0:T(8,128)(2,1)} %refs_0_.1) | copy-start | bytes 983044
  13.3 0.7 copy-start.4
  14.0 0.7 copy-start.8
  14.8 28.7 %copy-start.3 = (bf16[1,640,256]{2,1,0:T(8,128)(2,1)}, bf16[1,640,256]{2,1,0:T(8,128)(2,1)S(1)}, u32[]{:S(2)}) copy-start(bf16[1,640,256]{2,1,0:T(8,128)(2,1)S(1)} %get-tuple-element.95.refs_3_.refs_15_) | copy-start | bytes 983044
  14.8 28.7 %copy-start.5 = (bf16[1,640,256]{2,1,0:T(8,128)(2,1)}, bf16[1,640,256]{2,1,0:T(8,128)(2,1)S(1)}, u32[]{:S(2)}) copy-start(bf16[1,640,256]{2,1,0:T(8,128)(2,1)S(1)} %get-tuple-element.105.refs_1_.refs_13_) | copy-start | bytes 983044
  14.8 28.7 %copy-start.6 = (bf16[1,640,256]{2,1,0:T(8,128)(2,1)}, bf16[1,640,256]{2,1,0:T(8,128)(2,1)S(1)}, u32[]{:S(2)}) copy-start(bf16[1,640,256]{2,1,0:T(8,128)(2,1)S(1)} %get-tuple-element.106.refs_2_.refs_14_) | copy-start | bytes 983044
  14.8 28.7 %copy-start.7 = (bf16[1,640,256]{2,1,0:T(8,128)(2,1)}, bf16[1,640,256]{2,1,0:T(8,128)(2,1)S(1)}, u32[]{:S(2)}) copy-start(bf16[1,640,256]{2,1,0:T(8,128)(2,1)S(1)} %get-tuple-element.107.refs_3_.refs_15_) | copy-start | bytes 983044
  14.8 16.2 %copy-start = (bf16[1,640,512]{2,1,0:T(8,128)(2,1)S(1)}, bf16[1,640,512]{2,1,0:T(8,128)(2,1)}, u32[]{:S(2)}) copy-start(bf16[1,640,512]{2,1,0:T(8,128)(2,1)} %get-tuple-element.101.refs_2_.refs_8_) | copy-start | bytes 1966084
  14.8 16.2 %copy-start.1 = (bf16[1,640,512]{2,1,0:T(8,128)(2,1)S(1)}, bf16[1,640,512]{2,1,0:T(8,128)(2,1)}, u32[]{:S(2)}) copy-start(bf16[1,640,512]{2,1,0:T(8,128)(2,1)} %get-tuple-element.102.refs_3_.refs_9_) | copy-start | bytes 1966084
  43.4 13.4 %copy-start.2 = (bf16[1,640,512]{2,1,0:T(8,128)(2,1)S(1)}, bf16[1,640,512]{2,1,0:T(8,128)(2,1)}, u32[]{:S(2)}) copy-start(bf16[1,640,512]{2,1,0:T(8,128)(2,1)} %get-tuple-element.113.refs_2_.refs_8_) | copy-start | bytes 1966084
  139.4 28.5 %copy-start.9 = (f32[80,1536]{1,0:T(8,128)S(1)}, f32[80,1536]{1,0:T(8,128)}, u32[]{:S(2)}) copy-start(f32[80,1536]{1,0:T(8,128)} %get-tuple-element.154.refs_3_) | copy-start | bytes 1474564
  167.8 1.0 copy-start.10
  214.4 3.0 %copy-start.18 = (bf16[2,256,640]{2,1,0:T(8,128)(2,1)S(1)}, bf16[2,256,640]{2,1,0:T(8,128)(2,1)}, u32[]{:S(2)}) copy-start(bf16[2,256,640]{2,1,0:T(8,128)(2,1)} %get-tuple-element.169) | copy-start | bytes 1966084
  217.3 1.7 copy-start.17
